TPU v7x, 32 devices: a whole 2x2x4 slice. The times are simulated.
32 devices in a mesh: gx: 8 (over y, x, core), gy: 4 (over z).
Axes of the slice: x: 2, y: 2, z: 4, core: 2. Of those that a mesh axis runs over, the one named last changes fastest.
Arguments:
- state_now: float32 [32, 128, 4096], P(('gx', 'gy')), may hold values from -6 to 6
- state_prev: float32 [32, 128, 4096], P(('gx', 'gy')), may hold values from -6 to 6
- pml_flags: int32 [32], P(('gx', 'gy')), may hold values 0 or 1
- interfaces: int32 [64, 6], P(('gx', 'gy')), may hold values from -16 to 16, as said below
Outputs:
- new_state: float32 [32, 128, 4096], P(('gx', 'gy'))
- face_pressure: float32 [32, 6, 4096], P(('gx', 'gy'))
Inputs may be any that keep to these rules, and one draw needn't show every extreme that they name: `interfaces`: column 0 and column 1 are always 0 (each device holds one box); column 1 names the box of the device one step further along gx and g = column 2 steps across gy; g is -1, 0 or 1 and that device exists whenever column 5 is 1. Columns 3 and 4 are offsets from -16 to 16. Column 5 is 0 exactly on the rows of the last index of gx, which join nothing, and 1 elsewhere.
All inputs are finite; a program needn't handle non-finite values. No bound on the sum of `pml_flags` on one device may be relied on, other than what follows from the above.
Results may differ from a plain program's by a relative error of at most 0.0003.
Values sent between devices are 32-bit elements; how exact they have to be, the bound alone decides.
No kernel may reach another device: no remote copies, remote signals or barrier semaphores. Data moves between devices by JAX's collectives and lax.ppermute only.
A program may use at most 128 MiB of HBM per device.

v0:
```python
import functools
import math

import jax
import jax.numpy as jnp
import ml_dtypes
import numpy as np
from jax import lax
from jax.experimental import pallas as pl
from jax.experimental.pallas import tpu as pltpu
from jax.sharding import PartitionSpec as P

STEPS = 3
OFF = 16
COURANT = 0.4
DAMPING = 0.5
STENCIL = (-490.0, 270.0, -27.0, 2.0)
BLEND = ((1.5, -0.15, 1.0 / 90.0), (-0.15, 1.0 / 90.0, 0.0), (1.0 / 90.0, 0.0, 0.0))
SHIFTS = (-1, 0, 1)
CHUNK = 512
BF16 = ml_dtypes.bfloat16


def cosine_basis(count):
    freqs = np.arange(count)[:, None]
    cells = np.arange(count)[None, :]
    weight = np.where(freqs == 0, np.sqrt(1.0 / count), np.sqrt(2.0 / count))
    return weight * np.cos(math.pi * freqs * (cells + 0.5) / count)


def halves(values):
    high = values.astype(BF16)
    return high, (values - high.astype(np.float64)).astype(BF16)


def twice(block):
    zero = np.zeros_like(block)
    return np.block([[block, zero], [zero, block]])


def banded(count):
    distance = np.abs(np.arange(count)[:, None] - np.arange(count)[None, :])
    weights = np.zeros((count, count))
    for near in (1, 2, 3):
        weights[distance == near] = STENCIL[near]
    return weights


@functools.lru_cache(maxsize=None)
def make_tables(s0, side):
    along = cosine_basis(s0)
    cross = cosine_basis(side)
    wave = (
        ((math.pi * np.arange(s0) / s0) ** 2)[:, None, None]
        + ((math.pi * np.arange(side) / side) ** 2)[None, :, None]
        + ((math.pi * np.arange(side) / side) ** 2)[None, None, :]
    )
    rooted = np.sqrt(wave)
    safe = np.where(wave > 0.0, wave, 1.0)
    gain = np.where(
        wave > 0.0, 4.0 * np.sin(0.5 * COURANT * rooted) ** 2 / safe, COURANT * COURANT
    )
    twice_cosine = 2.0 * np.cos(COURANT * rooted)
    parity = np.arange(s0) % 2
    face = np.zeros((8, s0))
    for r in range(3):
        face[r] = along[:, r] * (parity == 0)
        face[3 + r] = along[:, r] * (parity == 1)
    face_high, face_low = halves(face)
    zero = np.zeros_like(face_low)
    collect = np.block([[face_high, face_high], [face_low, zero]])
    inject = np.concatenate([face_high.T, face_high.T, face_low.T, zero.T], axis=1)
    order = np.concatenate([np.arange(0, side, 2), np.arange(1, side, 2)])
    coupled = []
    for r in range(3):
        for s in range(r, 3):
            parts = [
                np.einsum("k,kab,k->ab", face[3 * o + r], gain, face[3 * o + s])[order] for o in (0, 1)
            ]
            coupled.append(np.concatenate(parts, axis=1))
    forward_one = np.concatenate([*([halves(cross[order])[0]] * 2), halves(cross[order])[1]], axis=1)
    inverse = cross[order].T
    inverse_one = np.concatenate([*([halves(inverse)[0]] * 2), halves(inverse)[1]], axis=1)
    forward_two = np.concatenate([*([halves(twice(cross.T))[0]] * 2), halves(twice(cross.T))[1]], axis=0)
    inverse_two = np.concatenate([*([halves(twice(cross))[0]] * 2), halves(twice(cross))[1]], axis=0)
    rate = DAMPING * ((np.arange(s0) + 0.5) / s0) ** 2
    first = (2.0 + COURANT * COURANT * 3.0 * STENCIL[0] / 180.0) / (1.0 + rate)
    second = -(1.0 - rate) / (1.0 + rate)
    third = COURANT * COURANT / (1.0 + rate)
    rows = [np.broadcast_to(v[:, None], (s0, 128)) for v in (first, second, third)]
    down = np.concatenate([banded(s0)] * 2, axis=1).astype(BF16)
    inside = np.concatenate([twice(banded(side))] * 2, axis=0).astype(BF16)
    face_third = np.stack(
        [np.concatenate([np.full(side, third[r]), np.full(side, third[s0 - 1 - r])]) for r in range(3)]
    )
    face_third = np.concatenate([face_third, np.zeros((5, 2 * side))])
    f32 = np.float32
    return {
        "cosine": twice_cosine.reshape(s0, side * side).astype(f32),
        "gain": gain.reshape(s0, side * side).astype(f32),
        "collect": collect,
        "inject": inject,
        "coupled": np.concatenate(coupled, axis=0).astype(f32),
        "forward_one": forward_one,
        "forward_two": forward_two,
        "inverse_one": inverse_one,
        "inverse_two": inverse_two,
        "rows": np.concatenate(rows, axis=0).astype(f32),
        "down": down,
        "inside": inside,
        "face_third": face_third.astype(f32),
    }


def pairing(nx, ny, parity, across):
    taken = {}
    for x in range(parity, nx - 1, 2):
        for y in range(ny):
            if 0 <= y + across < ny:
                taken[(x, y)] = (x + 1, y + across)
                taken[(x + 1, y + across)] = (x, y)
    rest = [(x, y) for x in range(nx) for y in range(ny) if (x, y) not in taken]
    while len(rest) > 1:
        x, y = rest.pop(0)
        mate = min(rest, key=lambda d: (abs(d[1] - y) + abs(d[0] // 2 - x // 2), d))
        if parity == 1 and x == 0:
            wrapped = [d for d in rest if d == (nx - 1, y - across)]
            mate = wrapped[0] if wrapped else mate
        rest.remove(mate)
        taken[(x, y)] = mate
        taken[mate] = (x, y)
    return [(x * ny + y, u * ny + v) for (x, y), (u, v) in sorted(taken.items())]


def left_lanes(shape):
    return lax.broadcasted_iota(jnp.int32, shape, len(shape) - 1) < shape[-1] // 2


def turned(block):
    return pltpu.roll(block, block.shape[-1] // 2, block.ndim - 1)


def two_halves(block):
    high = block.astype(jnp.bfloat16)
    low = (block - high.astype(jnp.float32)).astype(jnp.bfloat16)
    return high, low


def product(a, b):
    return jnp.dot(a, b, preferred_element_type=jnp.float32)


def over_rows(table, block):
    high, low = two_halves(block)
    return product(table, jnp.concatenate([high, low, high], axis=0))


def over_lanes(block, table):
    high, low = two_halves(block)
    return product(jnp.concatenate([high, low, high], axis=1), table)


def beside(planes):
    side = planes.shape[0] // 3
    return jnp.concatenate([planes[r * side : (r + 1) * side] for r in range(3)], axis=1)


def below(planes):
    wide = planes.shape[1] // 3
    return jnp.concatenate([planes[:, r * wide : (r + 1) * wide] for r in range(3)], axis=0)


def sum_difference(block):
    other = turned(block)
    return jnp.where(left_lanes(block.shape), block + other, other - block)


def mirrored_inverse(modes, inverse_one, inverse_two):
    cells = over_rows(inverse_one[...], beside(over_lanes(modes, inverse_two[...])))
    return sum_difference(below(cells))


def mirrored_forward(planes, forward_one, forward_two):
    cells = sum_difference(planes)
    return over_lanes(below(over_rows(forward_one[...], beside(cells))), forward_two[...])


def weave(first, second):
    left = left_lanes(first.shape)
    return jnp.where(left, first, turned(second)), jnp.where(left, turned(first), second)


def blended(planes):
    return [
        sum(BLEND[d][e] * planes[e] for e in range(3) if BLEND[d][e] != 0.0) for d in range(3)
    ]


def emit_payloads(layers, listed, place, outs, pads):
    side = layers.shape[0] // 3
    half = side // 2
    wide = layers.shape[1]
    left = left_lanes((half, wide))
    planes = [layers[r * side : (r + 1) * side] for r in range(3)]
    low = [jnp.where(left, p[:half], turned(p[half:])) for p in planes]
    low = jnp.concatenate(low, axis=0)
    whole = left_lanes((side, wide))
    for r, plane in enumerate(blended(planes)):
        pads[0, r, OFF : OFF + side] = jnp.where(whole, turned(plane), 0.0)
    packed = []
    for s in range(listed.shape[0]):
        start = OFF + listed[s, 3]
        roll = (wide - listed[s, 4]) % wide
        opposite = (wide + half * 2 - listed[s, 4]) % wide
        parts = []
        for r in range(3):
            top = pltpu.roll(pads[0, r, pl.ds(start, half)], roll, 1)
            bottom = pltpu.roll(pads[0, r, pl.ds(start + half, half)], opposite, 1)
            parts.append(jnp.where(left, top, bottom))
        packed.append(jnp.concatenate(parts, axis=0))
    even = place[0] == 1
    for i, g in enumerate(SHIFTS):
        force = jnp.zeros_like(low)
        for s in range(listed.shape[0]):
            wanted = (listed[s, 2] == g) & (listed[s, 5] != 0)
            force = force + jnp.where(wanted, packed[s], 0.0)
        outs[i][...] = jnp.where(even, force, low)
        outs[3 + i][...] = jnp.where(even, low, force)


def clear_pads(pads):
    side = pads.shape[2] - 2 * OFF
    blank = jnp.zeros((OFF, pads.shape[3]), jnp.float32)
    for n in range(pads.shape[0]):
        for r in range(3):
            pads[n, r, 0:OFF] = blank
            pads[n, r, OFF + side : 2 * OFF + side] = blank


def take_forces(arrived, listed, place, pads):
    wide = arrived[0].shape[1]
    half = arrived[0].shape[0] // 3
    side = 2 * half
    left = left_lanes((half, wide))
    even = place[0] == 1
    lows = [jnp.where(even, arrived[i][...], arrived[3 + i][...]) for i in range(3)]
    pushes = [jnp.where(even, arrived[3 + i][...], arrived[i][...]) for i in range(3)]
    pushed = jnp.zeros_like(lows[0])
    for i in range(3):
        pushed = pushed + jnp.where(place[1 + i] == 1, pushes[i], 0.0)
    high = [None] * 3
    for s in range(listed.shape[0]):
        g = listed[s, 2]
        chosen = jnp.where(g == 0, lows[1], jnp.where(g < 0, lows[0], lows[2]))
        chosen = jnp.where(listed[s, 5] != 0, chosen, 0.0)
        for r in range(3):
            part = chosen[r * half : (r + 1) * half]
            pads[1 + s, r, OFF : OFF + half] = jnp.where(left, part, 0.0)
            pads[1 + s, r, OFF + half : OFF + side] = jnp.where(left, turned(part), 0.0)
        start = OFF - listed[s, 3]
        roll = (listed[s, 4] + wide + side) % wide
        for r in range(3):
            moved = pltpu.roll(pads[1 + s, r, pl.ds(start, side)], roll, 1)
            high[r] = moved if high[r] is None else high[r] + moved
    high = blended(high)
    planes = []
    for r in range(3):
        part = pushed[r * half : (r + 1) * half]
        lower = jnp.concatenate([part, turned(part)], axis=0)
        planes.append(jnp.where(left_lanes((side, wide)), lower, high[r]))
    return jnp.concatenate(planes, axis=0)


def modal_response(force_modes, coupled):
    side = force_modes.shape[0] // 3
    planes = [force_modes[r * side : (r + 1) * side] for r in range(3)]
    index, n = {}, 0
    for r in range(3):
        for s in range(r, 3):
            index[r, s] = index[s, r] = n
            n += 1
    rows = []
    for r in range(3):
        total = None
        for s in range(3):
            i = index[r, s]
            term = coupled[i * side : (i + 1) * side, :] * planes[s]
            total = term if total is None else total + term
        rows.append(total)
    return jnp.concatenate(rows, axis=0)


def tile_count(ref):
    return ref.shape[1] // 128


def planes_of_modes(gathered, tiles):
    planes = []
    for r in range(3):
        planes += weave(
            gathered[r * tiles : (r + 1) * tiles, :], gathered[(3 + r) * tiles : (4 + r) * tiles, :]
        )
    return jnp.concatenate(planes, axis=0)


def collected(block, collect):
    high, low = two_halves(block)
    both = product(collect[...], jnp.concatenate([high, low], axis=0))
    return both[0:8] + both[8:16]


def scatter_tiles(rows, gathered, column):
    tiles = gathered.shape[0] // 8
    for i in range(rows.shape[1] // 128):
        gathered[pl.ds(column // 128 + i, 8, stride=tiles), :] = rows[:, i * 128 : (i + 1) * 128]


def gather_tiles(gathered, column, width):
    tiles = gathered.shape[0] // 8
    return jnp.concatenate(
        [gathered[pl.ds(column // 128 + i, 8, stride=tiles), :] for i in range(width // 128)], axis=1
    )


def pml_planes(state, gathered, woven):
    s0 = state.shape[0]
    tiles = tile_count(state)
    for start, base in ((0, 0), (s0 - 8, 8 * tiles)):
        for J in range(tiles):
            gathered[pl.ds(base + J, 8, stride=tiles), :] = state[
                start : start + 8, J * 128 : (J + 1) * 128
            ]
    for r in range(3):
        high = (8 + 7 - r) * tiles
        first, second = weave(
            gathered[r * tiles : (r + 1) * tiles, :], gathered[high : high + tiles, :]
        )
        woven[pl.ds(r * 2 * tiles, tiles, stride=2), :] = first
        woven[pl.ds(r * 2 * tiles + 1, tiles, stride=2), :] = second
    return woven[...]


def low_high_rows(planes, woven, tiles):
    woven[...] = planes
    rows = []
    for r in range(3):
        first = woven[pl.ds(r * 2 * tiles, tiles, stride=2), :]
        second = woven[pl.ds(r * 2 * tiles + 1, tiles, stride=2), :]
        rows.append(weave(first, second))
    return rows


def spread_pml_forces(planes, gathered, woven):
    tiles = gathered.shape[0] // 16
    rows = low_high_rows(planes, woven, tiles)
    blank = jnp.zeros((tiles, 128), jnp.float32)
    for s in range(8):
        gathered[s * tiles : (s + 1) * tiles, :] = rows[s][0] if s < 3 else blank
        gathered[(8 + s) * tiles : (9 + s) * tiles, :] = rows[7 - s][1] if s > 4 else blank


def spread_modal_forces(modes, gathered):
    tiles = gathered.shape[0] // 16
    side = modes.shape[0] // 3
    half = side // 2
    blank = jnp.zeros((tiles, 128), jnp.float32)
    for r in range(3):
        plane = modes[r * side : (r + 1) * side]
        even, odd = weave(plane[:half], plane[half:])
        gathered[r * tiles : (r + 1) * tiles, :] = even
        gathered[(3 + r) * tiles : (4 + r) * tiles, :] = odd
    for s in (6, 7):
        gathered[s * tiles : (s + 1) * tiles, :] = blank


def injected(gathered, inject, column, width):
    tiles = gathered.shape[0] // 16
    rows = jnp.concatenate(
        [gathered[pl.ds(column // 128 + i, 8, stride=tiles), :] for i in range(width // 128)], axis=1
    )
    high = rows.astype(jnp.bfloat16).astype(jnp.float32)
    stacked = jnp.concatenate([high, rows - high, high, jnp.zeros_like(rows)], axis=0)
    return product(inject[...], stacked.astype(jnp.bfloat16))


def pml_rows(gathered, column, width, base):
    tiles = gathered.shape[0] // 16
    return jnp.concatenate(
        [
            gathered[pl.ds(base * tiles + column // 128 + i, 8, stride=tiles), :]
            for i in range(width // 128)
        ],
        axis=1,
    )


def wide(rows, width):
    return jnp.concatenate([rows] * (width // 128), axis=1)


def stencil_sums(state, column, width, down, inside):
    total = state.shape[1]
    tiles = width // 128
    strip = state[:, column : column + width]
    high, low = two_halves(strip)
    sums = product(down[...], jnp.concatenate([high, low], axis=0))
    rows = [
        product(
            jnp.concatenate(
                [high[:, i * 128 : (i + 1) * 128], low[:, i * 128 : (i + 1) * 128]], axis=1
            ),
            inside[...],
        )
        for i in range(tiles)
    ]
    sums = sums + jnp.concatenate(rows, axis=1)

    def tile(i):
        at = column + i * 128
        if at < 0 or at >= total:
            return None
        return state[:, at : at + 128]

    near = {i: tile(i) for i in range(-2, tiles + 2)}
    spun = {i: None if v is None else turned(v) for i, v in near.items()}
    left = left_lanes((state.shape[0], 128))

    def between(i):
        a, b = spun.get(i - 1), spun.get(i)
        a = jnp.zeros(left.shape, jnp.float32) if a is None else a
        b = jnp.zeros(left.shape, jnp.float32) if b is None else b
        return jnp.where(left, a, b)

    def plus(a, b):
        return b if a is None else a if b is None else a + b

    moved = {i: between(i) for i in range(-1, tiles + 2)}
    across = [
        STENCIL[1] * (moved[i] + moved[i + 1])
        + STENCIL[2] * plus(near[i - 1], near[i + 1])
        + STENCIL[3] * (moved[i - 1] + moved[i + 2])
        for i in range(tiles)
    ]
    return sums + jnp.concatenate(across, axis=1)


def start_kernel(flag, listed, place, state, collect, inverse_one, inverse_two, *rest):
    outs, (layers, pads, gathered, woven) = rest[:6], rest[6:]
    clear_pads(pads)

    @pl.when(flag[0] > 0)
    def _():
        layers[...] = pml_planes(state, gathered, woven)

    @pl.when(flag[0] <= 0)
    def _():
        for column in range(0, state.shape[1], CHUNK):
            rows = collected(state[:, column : column + CHUNK], collect)
            scatter_tiles(rows, gathered.at[0 : 8 * tile_count(state)], column)
        modes = planes_of_modes(gathered, tile_count(state))
        layers[...] = mirrored_inverse(modes, inverse_one, inverse_two)

    emit_payloads(layers[...], listed, place, outs, pads)


def free_kernel(first, keep, flag, *refs):
    refs = list(refs)
    forces = None if first else refs.pop(0)
    current, before, cosine = refs[:3]
    refs = refs[3:]
    gain, inject = (None, None) if first else (refs.pop(0), refs.pop(0))
    collect, inverse_one, inverse_two, rows, down, inside = refs[:6]
    refs = refs[6:]
    whole = refs.pop(0) if keep else current
    free, layers, gathered, woven = refs
    s0, total = current.shape
    tiles = total // 128

    @pl.when(flag[0] > 0)
    def _():
        if keep:
            spread_pml_forces(forces[...], gathered, woven)
            for column in range(0, total, CHUNK):
                span = slice(column, column + CHUNK)
                whole[8 : s0 - 8, span] = current[8 : s0 - 8, span]
                for at, base in ((0, 0), (s0 - 8, 8)):
                    scale = wide(rows[2 * s0 + at : 2 * s0 + at + 8, :], CHUNK)
                    whole[at : at + 8, span] = current[at : at + 8, span] + scale * pml_rows(
                        gathered, column, CHUNK, base
                    )
        for column in range(0, total, CHUNK):
            span = slice(column, column + CHUNK)
            sums = stencil_sums(whole, column, CHUNK, down, inside)
            free[:, span] = (
                wide(rows[0:s0, :], CHUNK) * whole[:, span]
                + wide(rows[s0 : 2 * s0, :], CHUNK) * before[:, span]
                + wide(rows[2 * s0 : 3 * s0, :], CHUNK) * (sums * (1.0 / 180.0))
            )
        layers[...] = pml_planes(free, gathered, woven)

    @pl.when(flag[0] <= 0)
    def _():
        if keep:
            spread_modal_forces(forces[...], gathered)
        parts = []
        for column in range(0, total, CHUNK):
            span = slice(column, column + CHUNK)
            value = current[:, span]
            if keep:
                value = value + gain[:, span] * injected(gathered, inject, column, CHUNK)
                whole[:, span] = value
            value = cosine[:, span] * value - before[:, span]
            free[:, span] = value
            parts.append(collected(value, collect))
        for i, part in enumerate(parts):
            scatter_tiles(part, gathered.at[0 : 8 * tiles], i * CHUNK)
        layers[...] = mirrored_inverse(planes_of_modes(gathered, tiles), inverse_one, inverse_two)


def advance_layers(flag, listed, place, arrived, layers, tables, forces, next_layers, pads):
    coupled, forward_one, forward_two, inverse_one, inverse_two, face_third = tables
    clear_pads(pads)
    push = take_forces(arrived, listed, place, pads)
    side = push.shape[0] // 3

    @pl.when(flag[0] > 0)
    def _():
        forces[...] = push
        for r in range(3):
            span = slice(r * side, (r + 1) * side)
            next_layers[span, :] = layers[span, :] + face_third[r : r + 1, :] * push[span]

    @pl.when(flag[0] <= 0)
    def _():
        modes = mirrored_forward(push, forward_one, forward_two)
        forces[...] = modes
        answer = mirrored_inverse(modal_response(modes, coupled), inverse_one, inverse_two)
        next_layers[...] = layers[...] + answer


def force_kernel(flag, listed, place, *refs):
    arrived, layers, tables = refs[:6], refs[6], refs[7:13]
    forces, outs, (next_layers, pads) = refs[13], refs[14:20], refs[20:]
    advance_layers(flag, listed, place, arrived, layers, tables, forces, next_layers, pads)
    emit_payloads(next_layers[...], listed, place, outs, pads)


def last_kernel(flag, listed, place, *refs):
    arrived, layers, tables = refs[:6], refs[6], refs[7:13]
    free, gain, inject, rows = refs[13:17]
    state, faces, forces, next_layers, pads, gathered, woven = refs[17:]
    advance_layers(flag, listed, place, arrived, layers, tables, forces, next_layers, pads)
    s0, total = free.shape
    tiles = total // 128

    @pl.when(flag[0] > 0)
    def _():
        spread_pml_forces(forces[...], gathered, woven)
        state[8 : s0 - 8, :] = free[8 : s0 - 8, :]
        for column in range(0, total, CHUNK):
            span = slice(column, column + CHUNK)
            for at, base in ((0, 0), (s0 - 8, 8)):
                scale = wide(rows[2 * s0 + at : 2 * s0 + at + 8, :], CHUNK)
                state[at : at + 8, span] = free[at : at + 8, span] + scale * pml_rows(
                    gathered, column, CHUNK, base
                )

    @pl.when(flag[0] <= 0)
    def _():
        spread_modal_forces(forces[...], gathered)
        for column in range(0, total, CHUNK):
            span = slice(column, column + CHUNK)
            state[:, span] = free[:, span] + gain[:, span] * injected(gathered, inject, column, CHUNK)

    shown = low_high_rows(next_layers[...], woven, tiles)
    for r in range(3):
        gathered[r * tiles : (r + 1) * tiles, :] = shown[r][0]
        gathered[(3 + r) * tiles : (4 + r) * tiles, :] = shown[r][1]
    for J in range(tiles):
        faces[:, J * 128 : (J + 1) * 128] = gathered[pl.ds(J, 8, stride=tiles), :][0:6]


SCALAR = pl.BlockSpec(memory_space=pltpu.SMEM)
BLOCK = pl.BlockSpec(memory_space=pltpu.VMEM)


def run(body, scalars, blocks, outs, scratch, flops=0):
    moved = sum(b.size * b.dtype.itemsize for b in blocks)
    return pl.pallas_call(
        body,
        out_shape=[jax.ShapeDtypeStruct(s, jnp.float32) for s in outs],
        in_specs=[SCALAR] * len(scalars) + [BLOCK] * len(blocks),
        out_specs=[BLOCK] * len(outs),
        scratch_shapes=[pltpu.VMEM(s, jnp.float32) for s in scratch],
        compiler_params=pltpu.CompilerParams(vmem_limit_bytes=32 * 1024 * 1024),
        cost_estimate=pl.CostEstimate(flops=flops, bytes_accessed=moved, transcendentals=0),
    )(*scalars, *blocks)


def local(nx, ny, state_now, state_prev, pml_flags, interfaces):
    _, s0, cross = state_now.shape
    side = math.isqrt(cross)
    t = {k: jnp.asarray(v) for k, v in make_tables(s0, side).items()}
    tiles = cross // 128
    now, before = state_now[0], state_prev[0]
    gx, gy = lax.axis_index("gx"), lax.axis_index("gy")
    reach = [(gx > 0) & (gy - g >= 0) & (gy - g < ny) for g in SHIFTS]
    place = jnp.stack([gx % 2 == 0, *reach]).astype(jnp.int32)
    scalars = (pml_flags, interfaces, place)
    planes = (3 * side, 128)
    packed = (3 * side // 2, 128)
    pads = (1 + interfaces.shape[0], 3, side + 2 * OFF, 128)
    gathered = (16 * tiles, 128)
    routes = [pairing(nx, ny, parity, g) for parity in (0, 1) for g in SHIFTS]
    send_order = (5, 3, 4, 2, 0, 1)

    def exchange(payloads):
        arrived = [None] * 6
        for i in send_order:
            arrived[i] = lax.ppermute(payloads[i], ("gx", "gy"), routes[i])
        return arrived

    payloads = run(
        start_kernel,
        scalars,
        (now, t["collect"], t["inverse_one"], t["inverse_two"]),
        [packed] * 6,
        [planes, pads, gathered, planes],
    )
    tables = [
        t[k]
        for k in ("coupled", "forward_one", "forward_two", "inverse_one", "inverse_two", "face_third")
    ]
    shared = [t[k] for k in ("collect", "inverse_one", "inverse_two", "rows", "down", "inside")]
    forces = None
    current = now
    for step in range(STEPS):
        arrived = exchange(payloads)
        full = (s0, cross)
        if step == 0:
            free, layers = run(
                functools.partial(free_kernel, True, False),
                scalars[:1],
                (current, before, t["cosine"], *shared),
                [full, planes],
                [gathered, planes],
                flops=10**9,
            )
        else:
            whole, free, layers = run(
                functools.partial(free_kernel, False, True),
                scalars[:1],
                (forces, free, current, t["cosine"], t["gain"], t["inject"], *shared),
                [full, full, planes],
                [gathered, planes],
                flops=10**9,
            )
            current = whole
        if step < STEPS - 1:
            forces, *payloads = run(
                force_kernel,
                scalars,
                (*arrived, layers, *tables),
                [planes] + [packed] * 6,
                [planes, pads],
            )
        else:
            state, faces = run(
                last_kernel,
                scalars,
                (*arrived, layers, *tables, free, t["gain"], t["inject"], t["rows"]),
                [full, (6, cross)],
                [planes, planes, pads, gathered, planes],
            )
    return state[None], faces[None]


def solution(mesh):
    placed = (
        P(("gx", "gy"), None, None),
        P(("gx", "gy"), None, None),
        P(("gx", "gy")),
        P(("gx", "gy"), None),
    )
    return jax.shard_map(
        functools.partial(local, mesh.shape["gx"], mesh.shape["gy"]),
        mesh=mesh,
        in_specs=placed,
        out_specs=(P(("gx", "gy"), None, None), P(("gx", "gy"), None, None)),
        check_vma=False,
    )
```

profile of v0, /device:TPU:0, one launch (start us, length us, event | category | flops | bytes accessed | tf_op | source)
XLA Modules:
  0.0 52.8 jit_solution(2424427791318771827)
XLA Ops:
  0.6 0.0 copy-start.6
  1.3 0.1 add_convert_fusion.place
  1.4 1.6 %copy-done = f32[1,128,4096]{2,1,0:T(8,128)S(1)} copy-done((f32[1,128,4096]{2,1,0:T(8,128)S(1)}, f32[1,128,4096]{2,1,0:T(8,128)}, u32[]{:S(2)}) %copy-start) | copy-done | bytes 2097176
  3.0 0.9 %copy-done.5 = bf16[384,128]{1,0:T(8,128)(2,1)S(1)} copy-done((bf16[384,128]{1,0:T(8,128)(2,1)S(1)}, bf16[384,128]{1,0:T(8,128)(2,1)}, u32[]{:S(2)}) %copy-start.5) | copy-done | bytes 98328
  3.9 0.8 %copy-done.11 = bf16[64,192]{1,0:T(8,128)(2,1)S(1)} copy-done((bf16[64,192]{1,0:T(8,128)(2,1)S(1)}, bf16[64,192]{1,0:T(8,128)(2,1)}, u32[]{:S(2)}) %copy-start.11) | copy-done | bytes 24600
  4.7 0.7 %copy-done.18 = bf16[16,256]{1,0:T(8,128)(2,1)S(1)} copy-done((bf16[16,256]{1,0:T(8,128)(2,1)S(1)}, bf16[16,256]{1,0:T(8,128)(2,1)}, u32[]{:S(2)}) %copy-start.18) | copy-done | bytes 8216
  5.4 0.7 %copy-done.21 = s32[2,6]{1,0:T(2,128)S(1)} copy-done((s32[2,6]{1,0:T(2,128)S(1)}, s32[2,6]{1,0:T(2,128)}, u32[]{:S(2)}) %copy-start.21) | copy-done | bytes 72
  6.1 1.7 %shard_map.176 = (f32[96,128]{1,0:T(8,128)S(1)}, f32[96,128]{1,0:T(8,128)S(1)}, f32[96,128]{1,0:T(8,128)S(1)}, f32[96,128]{1,0:T(8,128)S(1)}, f32[96,128]{1,0:T(8,128)S(1)}, /*index=5*/f32[96,128]{1,0:T(8,128)S(1)}) custom-call(s32[1]{0:T(128)S(6)} %copy.20.flag, s32[2,6]{1,0:T(2,128)S(1)} %copy-done.21, s32[4]{0:T(128)S(1)} %add_convert_fusion.place, ...), custom_call_target="tpu_custom_call" | custom-call | bytes 2228224 | tf_op jit(solution)/shard_map/pallas_call | solution.py:589
  7.8 3.0 %collective-permute-start = (f32[96,128]{1,0:T(8,128)S(1)}, f32[96,128]{1,0:T(8,128)S(1)}, u32[]{:S(2)}, u32[]{:S(2)}) collective-permute-start(f32[96,128]{1,0:T(8,128)S(1)} %get-tuple-element.31), channel_id=1, source_target_pairs={{0,8},{1,4},{2,5},{3,6},{4,1},{5,2},{6,3},{7,15},{8,0},{9,12},{10,... | collective-permute-start | bytes 147464 | tf_op jit(solution)/shard_map/ppermute | solution.py:620
  10.8 0.2 collective-permute-start.1
  11.0 1.2 %collective-permute-start.2 = (f32[96,128]{1,0:T(8,128)S(1)}, f32[96,128]{1,0:T(8,128)S(1)}, u32[]{:S(2)}, u32[]{:S(2)}) collective-permute-start(f32[96,128]{1,0:T(8,128)S(1)} %get-tuple-element.33), channel_id=1, source_target_pairs={{0,5},{1,6},{2,7},{3,11},{4,12},{5,0},{6,1},{7,2},{8,13},{9,14},{1... | collective-permute-start | bytes 147464 | tf_op jit(solution)/shard_map/ppermute | solution.py:620
  12.1 2.4 %collective-permute-start.3 = (f32[96,128]{1,0:T(8,128)S(1)}, f32[96,128]{1,0:T(8,128)S(1)}, u32[]{:S(2)}, u32[]{:S(2)}) collective-permute-start(f32[96,128]{1,0:T(8,128)S(1)} %get-tuple-element.34), channel_id=1, source_target_pairs={{0,29},{1,30},{2,31},{3,11},{4,12},{5,8},{6,9},{7,10},{8,5},{9,6},... | collective-permute-start | bytes 147464 | tf_op jit(solution)/shard_map/ppermute | solution.py:620
  14.6 0.0 collective-permute-start.4
  14.6 1.7 %collective-permute-start.5 = (f32[96,128]{1,0:T(8,128)S(1)}, f32[96,128]{1,0:T(8,128)S(1)}, u32[]{:S(2)}, u32[]{:S(2)}) collective-permute-start(f32[96,128]{1,0:T(8,128)S(1)} %get-tuple-element.36), channel_id=1, source_target_pairs={{0,1},{1,0},{2,29},{3,30},{4,9},{5,10},{6,11},{7,15},{8,16},{9,4},... | collective-permute-start | bytes 147464 | tf_op jit(solution)/shard_map/ppermute | solution.py:620
  16.3 0.0 copy-start.3
  16.3 1.6 %copy-done.3 = f32[128,4096]{1,0:T(8,128)S(1)} copy-done((f32[128,4096]{1,0:T(8,128)S(1)}, f32[128,4096]{1,0:T(8,128)}, u32[]{:S(2)}) %copy-start.3) | copy-done | bytes 2097176
  17.9 0.9 %copy-done.7 = f32[384,128]{1,0:T(8,128)S(1)} copy-done((f32[384,128]{1,0:T(8,128)S(1)}, f32[384,128]{1,0:T(8,128)}, u32[]{:S(2)}) %copy-start.7) | copy-done | bytes 196632
  18.8 1.6 %copy-done.9 = f32[1,128,4096]{2,1,0:T(8,128)S(1)} copy-done((f32[1,128,4096]{2,1,0:T(8,128)S(1)}, f32[1,128,4096]{2,1,0:T(8,128)}, u32[]{:S(2)}) %copy-start.9) | copy-done | bytes 2097176
  20.4 0.8 %copy-done.15 = bf16[128,256]{1,0:T(8,128)(2,1)S(1)} copy-done((bf16[128,256]{1,0:T(8,128)(2,1)S(1)}, bf16[128,256]{1,0:T(8,128)(2,1)}, u32[]{:S(2)}) %copy-start.15) | copy-done | bytes 65560
  21.2 0.0 copy-start.22
  21.3 0.0 copy-start.2
  21.3 0.0 copy-start.4
  21.3 0.0 copy-start.16
  21.3 1.2 %shard_map.177 = (f32[128,4096]{1,0:T(8,128)S(1)}, f32[192,128]{1,0:T(8,128)S(1)}) custom-call(s32[1]{0:T(128)S(6)} %copy.20.flag, f32[128,4096]{1,0:T(8,128)S(1)} %bitcast.9, f32[128,4096]{1,0:T(8,128)S(1)} %bitcast.11, f32[128,4096]{1,0:T(8,128)S(1)} %copy-done.3, bf16[16,256]{1,0:T(8,128)(2,1)S(1)} %copy-done.19, bf16[64,192]{1,0:T(8,128)(2,1)S(1)} %copy-done.12, ...), custom_call_target="tpu_custom_call" | custom-call | flops 1000000000 | bytes 6750208 | tf_op jit(solution)/shard_map/pallas_call | solution.py:589
  22.5 0.0 collective-permute-done.1.refs_1_
  22.6 0.0 collective-permute-done.3.refs_3_
  22.6 0.0 collective-permute-done.4.refs_4_
  22.6 1.8 %shard_map.178 = (f32[192,128]{1,0:T(8,128)S(1)}, f32[96,128]{1,0:T(8,128)S(1)}, f32[96,128]{1,0:T(8,128)S(1)}, f32[96,128]{1,0:T(8,128)S(1)}, f32[96,128]{1,0:T...) custom-call(s32[1]{0:T(128)S(6)} %copy.20.flag, s32[2,6]{1,0:T(2,128)S(1)} %copy-done.22, ...), custom_call_target="tpu_custom_call" | custom-call | bytes 839680 | tf_op jit(solution)/shard_map/pallas_call | solution.py:589
  24.4 0.4 collective-permute-start.6
  24.9 0.1 collective-permute-start.7
  25.0 3.3 %collective-permute-start.8 = (f32[96,128]{1,0:T(8,128)S(1)}, f32[96,128]{1,0:T(8,128)S(1)}, u32[]{:S(2)}, u32[]{:S(2)}) collective-permute-start(f32[96,128]{1,0:T(8,128)S(1)} %get-tuple-element.40), channel_id=1, source_target_pairs={{0,5},{1,6},{2,7},{3,11},{4,12},{5,0},{6,1},{7,2},{8,13},{9,14},{1... | collective-permute-start | bytes 147464 | tf_op jit(solution)/shard_map/ppermute | solution.py:620
  28.3 0.1 collective-permute-start.10
  28.4 0.7 %collective-permute-done.6.refs_0_ = f32[96,128]{1,0:T(8,128)S(1)} collective-permute-done((f32[96,128]{1,0:T(8,128)S(1)}, f32[96,128]{1,0:T(8,128)S(1)}, u32[]{:S(2)}, u32[]{:S(2)}) %collective-permute-start.6) | collective-permute-done | bytes 49184 | tf_op jit(solution)/shard_map/ppermute | solution.py:620
  29.1 3.3 %collective-permute-start.11 = (f32[96,128]{1,0:T(8,128)S(1)}, f32[96,128]{1,0:T(8,128)S(1)}, u32[]{:S(2)}, u32[]{:S(2)}) collective-permute-start(f32[96,128]{1,0:T(8,128)S(1)} %get-tuple-element.43), channel_id=1, source_target_pairs={{0,1},{1,0},{2,29},{3,30},{4,9},{5,10},{6,11},{7,15},{8,16},{9,4},... | collective-permute-start | bytes 147464 | tf_op jit(solution)/shard_map/ppermute | solution.py:620
  32.4 2.3 %shard_map.179 = (f32[128,4096]{1,0:T(8,128)S(1)}, f32[128,4096]{1,0:T(8,128)S(1)}, f32[192,128]{1,0:T(8,128)S(1)}) custom-call(s32[1]{0:T(128)S(6)} %copy.20.flag, f32[192,128]{1,0:T(8,128)S(1)} %get-tuple-element.44.refs_0_, f32[128,4096]{1,0:T(8,128)S(1)} %get-tuple-element.45.refs_1_, f32[128,4096]{1,0:T(8,128)S(1)} %bitcast.10, ...), custom_call_target="tpu_custom_call" | custom-call | flops 1000000000 | bytes 8953856 | tf_op jit(solution)/shard_map/pallas_call | solution.py:589
  34.7 0.0 collective-permute-done.7.refs_1_
  34.7 0.0 collective-permute-done.8.refs_2_
  34.8 0.0 collective-permute-done.11.refs_5_
  34.8 1.8 %shard_map.180 = (f32[192,128]{1,0:T(8,128)S(1)}, f32[96,128]{1,0:T(8,128)S(1)}, f32[96,128]{1,0:T(8,128)S(1)}, f32[96,128]{1,0:T(8,128)S(1)}, f32[96,128]{1,0:T...) custom-call(s32[1]{0:T(128)S(6)} %copy.20.flag, s32[2,6]{1,0:T(2,128)S(1)} %copy-done.22, ...), custom_call_target="tpu_custom_call" | custom-call | bytes 839680 | tf_op jit(solution)/shard_map/pallas_call | solution.py:589
  36.6 0.1 collective-permute-start.12
  36.7 1.8 %collective-permute-start.13 = (f32[96,128]{1,0:T(8,128)S(1)}, f32[96,128]{1,0:T(8,128)S(1)}, u32[]{:S(2)}, u32[]{:S(2)}) collective-permute-start(f32[96,128]{1,0:T(8,128)S(1)} %get-tuple-element.48), channel_id=1, source_target_pairs={{0,4},{1,5},{2,6},{3,7},{4,0},{5,1},{6,2},{7,3},{8,12},{9,13},{10,... | collective-permute-start | bytes 147464 | tf_op jit(solution)/shard_map/ppermute | solution.py:620
  38.4 2.4 %collective-permute-start.14 = (f32[96,128]{1,0:T(8,128)S(1)}, f32[96,128]{1,0:T(8,128)S(1)}, u32[]{:S(2)}, u32[]{:S(2)}) collective-permute-start(f32[96,128]{1,0:T(8,128)S(1)} %get-tuple-element.49), channel_id=1, source_target_pairs={{0,5},{1,6},{2,7},{3,11},{4,12},{5,0},{6,1},{7,2},{8,13},{9,14},{1... | collective-permute-start | bytes 147464 | tf_op jit(solution)/shard_map/ppermute | solution.py:620
  40.8 0.0 collective-permute-start.15
  40.8 0.5 collective-permute-start.16
  41.4 3.6 %collective-permute-start.17 = (f32[96,128]{1,0:T(8,128)S(1)}, f32[96,128]{1,0:T(8,128)S(1)}, u32[]{:S(2)}, u32[]{:S(2)}) collective-permute-start(f32[96,128]{1,0:T(8,128)S(1)} %get-tuple-element.52), channel_id=1, source_target_pairs={{0,1},{1,0},{2,29},{3,30},{4,9},{5,10},{6,11},{7,15},{8,16},{9,4},... | collective-permute-start | bytes 147464 | tf_op jit(solution)/shard_map/ppermute | solution.py:620
  45.0 3.7 %shard_map.181 = (f32[128,4096]{1,0:T(8,128)}, f32[128,4096]{1,0:T(8,128)S(1)}, f32[192,128]{1,0:T(8,128)S(1)}) custom-call(s32[1]{0:T(128)S(6)} %copy.20.flag, f32[192,128]{1,0:T(8,128)S(1)} %get-tuple-element.53.refs_0_, f32[128,4096]{1,0:T(8,128)S(1)} %get-tuple-element.54.refs_1_, f32[128,4096]{1,0:T(8,128)S(1)} %get-tuple-element.55.refs_2_, ...), custom_call_target="tpu_custom_call" | custom-call | flops 1000000000 | bytes 8953856 | tf_op jit(solution)/shard_map/pallas_call | solution.py:589
  48.7 3.4 %shard_map.182 = (f32[128,4096]{1,0:T(8,128)}, f32[6,4096]{1,0:T(8,128)S(1)}) custom-call(s32[1]{0:T(128)S(6)} %copy.20.flag, s32[2,6]{1,0:T(2,128)S(1)} %copy-done.22, s32[4]{0:T(128)S(1)} %add_convert_fusion.place, f32[96,128]{1,0:T(8,128)S(1)} %collective-permute-done.12.refs_0_, f32[96,128]{1,0:T(8,128)S(1)} %collective-permute-done.13.refs_1_, ...), custom_call_target="tpu_custom_call" | custom-call | bytes 5238784 | tf_op jit(solution)/shard_map/pallas_call | solution.py:589
  52.1 0.7 %copy.19 = f32[1,6,4096]{2,0,1:T(1,128)} copy(f32[1,6,4096]{2,1,0:T(8,128)S(1)} %bitcast.12) | data formatting | bytes 196608
  (43 shorter events, 0.1 us)
Async XLA Ops:
  0.6 15.6 %copy-start.6 = (bf16[384,128]{1,0:T(8,128)(2,1)S(1)}, bf16[384,128]{1,0:T(8,128)(2,1)}, u32[]{:S(2)}) copy-start(bf16[384,128]{1,0:T(8,128)(2,1)} %constant.64.clone.inverse_two.refs_5_.refs_11_.refs_8_) | copy-start | bytes 294916
  1.4 1.6 %copy-start = (f32[1,128,4096]{2,1,0:T(8,128)S(1)}, f32[1,128,4096]{2,1,0:T(8,128)}, u32[]{:S(2)}) copy-start(f32[1,128,4096]{2,1,0:T(8,128)} %param.17) | copy-start | bytes 6291460
  3.0 0.9 %copy-start.5 = (bf16[384,128]{1,0:T(8,128)(2,1)S(1)}, bf16[384,128]{1,0:T(8,128)(2,1)}, u32[]{:S(2)}) copy-start(bf16[384,128]{1,0:T(8,128)(2,1)} %constant.64.clone.inverse_two.refs_5_.refs_11_.refs_8_) | copy-start | bytes 294916
  3.9 0.8 %copy-start.11 = (bf16[64,192]{1,0:T(8,128)(2,1)S(1)}, bf16[64,192]{1,0:T(8,128)(2,1)}, u32[]{:S(2)}) copy-start(bf16[64,192]{1,0:T(8,128)(2,1)} %constant.63.clone.inverse_one.refs_4_.refs_10_.refs_7_) | copy-start | bytes 73732
  4.7 0.7 %copy-start.18 = (bf16[16,256]{1,0:T(8,128)(2,1)S(1)}, bf16[16,256]{1,0:T(8,128)(2,1)}, u32[]{:S(2)}) copy-start(bf16[16,256]{1,0:T(8,128)(2,1)} %constant.58.clone.collect.refs_3_.refs_6_) | copy-start | bytes 24580
  5.4 0.7 %copy-start.21 = (s32[2,6]{1,0:T(2,128)S(1)}, s32[2,6]{1,0:T(2,128)}, u32[]{:S(2)}) copy-start(s32[2,6]{1,0:T(2,128)} %listed.7) | copy-start | bytes 148
  6.0 10.2 %copy-start.1 = (f32[1,128,4096]{2,1,0:T(8,128)S(1)}, f32[1,128,4096]{2,1,0:T(8,128)}, u32[]{:S(2)}) copy-start(f32[1,128,4096]{2,1,0:T(8,128)} %param.17) | copy-start | bytes 6291460
  6.0 10.2 %copy-start.12 = (bf16[64,192]{1,0:T(8,128)(2,1)S(1)}, bf16[64,192]{1,0:T(8,128)(2,1)}, u32[]{:S(2)}) copy-start(bf16[64,192]{1,0:T(8,128)(2,1)} %constant.63.clone.inverse_one.refs_4_.refs_10_.refs_7_) | copy-start | bytes 73732
  6.0 10.2 %copy-start.14 = (bf16[256,128]{1,0:T(8,128)(2,1)S(1)}, bf16[256,128]{1,0:T(8,128)(2,1)}, u32[]{:S(2)}) copy-start(bf16[256,128]{1,0:T(8,128)(2,1)} %constant.67.clone.refs_8_.refs_11_) | copy-start | bytes 196612
  6.1 10.2 %copy-start.19 = (bf16[16,256]{1,0:T(8,128)(2,1)S(1)}, bf16[16,256]{1,0:T(8,128)(2,1)}, u32[]{:S(2)}) copy-start(bf16[16,256]{1,0:T(8,128)(2,1)} %constant.58.clone.collect.refs_3_.refs_6_) | copy-start | bytes 24580
  7.8 6.8 %collective-permute-start = (f32[96,128]{1,0:T(8,128)S(1)}, f32[96,128]{1,0:T(8,128)S(1)}, u32[]{:S(2)}, u32[]{:S(2)}) collective-permute-start(f32[96,128]{1,0:T(8,128)S(1)} %get-tuple-element.31), channel_id=1, source_target_pairs={{0,8},{1,4},{2,5},{3,6},{4,1},{5,2},{6,3},{7,15},{8,0},{9,12},{10,... | collective-permute-start | bytes 147464 | tf_op jit(solution)/shard_map/ppermute | solution.py:620
  10.8 11.8 %collective-permute-start.1 = (f32[96,128]{1,0:T(8,128)S(1)}, f32[96,128]{1,0:T(8,128)S(1)}, u32[]{:S(2)}, u32[]{:S(2)}) collective-permute-start(f32[96,128]{1,0:T(8,128)S(1)} %get-tuple-element.32), channel_id=1, source_target_pairs={{0,4},{1,5},{2,6},{3,7},{4,0},{5,1},{6,2},{7,3},{8,12},{9,13},{10,... | collective-permute-start | bytes 147464 | tf_op jit(solution)/shard_map/ppermute | solution.py:620
  11.0 11.6 %collective-permute-start.2 = (f32[96,128]{1,0:T(8,128)S(1)}, f32[96,128]{1,0:T(8,128)S(1)}, u32[]{:S(2)}, u32[]{:S(2)}) collective-permute-start(f32[96,128]{1,0:T(8,128)S(1)} %get-tuple-element.33), channel_id=1, source_target_pairs={{0,5},{1,6},{2,7},{3,11},{4,12},{5,0},{6,1},{7,2},{8,13},{9,14},{1... | collective-permute-start | bytes 147464 | tf_op jit(solution)/shard_map/ppermute | solution.py:620
  12.1 10.4 %collective-permute-start.3 = (f32[96,128]{1,0:T(8,128)S(1)}, f32[96,128]{1,0:T(8,128)S(1)}, u32[]{:S(2)}, u32[]{:S(2)}) collective-permute-start(f32[96,128]{1,0:T(8,128)S(1)} %get-tuple-element.34), channel_id=1, source_target_pairs={{0,29},{1,30},{2,31},{3,11},{4,12},{5,8},{6,9},{7,10},{8,5},{9,6},... | collective-permute-start | bytes 147464 | tf_op jit(solution)/shard_map/ppermute | solution.py:620
  14.6 8.0 %collective-permute-start.4 = (f32[96,128]{1,0:T(8,128)S(1)}, f32[96,128]{1,0:T(8,128)S(1)}, u32[]{:S(2)}, u32[]{:S(2)}) collective-permute-start(f32[96,128]{1,0:T(8,128)S(1)} %get-tuple-element.35), channel_id=1, source_target_pairs={{0,28},{1,29},{2,30},{3,31},{4,8},{5,9},{6,10},{7,11},{8,4},{9,5},... | collective-permute-start | bytes 147464 | tf_op jit(solution)/shard_map/ppermute | solution.py:620
  14.6 8.0 %collective-permute-start.5 = (f32[96,128]{1,0:T(8,128)S(1)}, f32[96,128]{1,0:T(8,128)S(1)}, u32[]{:S(2)}, u32[]{:S(2)}) collective-permute-start(f32[96,128]{1,0:T(8,128)S(1)} %get-tuple-element.36), channel_id=1, source_target_pairs={{0,1},{1,0},{2,29},{3,30},{4,9},{5,10},{6,11},{7,15},{8,16},{9,4},... | collective-permute-start | bytes 147464 | tf_op jit(solution)/shard_map/ppermute | solution.py:620
  16.3 1.6 %copy-start.3 = (f32[128,4096]{1,0:T(8,128)S(1)}, f32[128,4096]{1,0:T(8,128)}, u32[]{:S(2)}) copy-start(f32[128,4096]{1,0:T(8,128)} %constant.56.clone.refs_2_.refs_3_) | copy-start | bytes 6291460
  17.9 0.9 %copy-start.7 = (f32[384,128]{1,0:T(8,128)S(1)}, f32[384,128]{1,0:T(8,128)}, u32[]{:S(2)}) copy-start(f32[384,128]{1,0:T(8,128)} %constant.65.clone.refs_6_.refs_9_.refs_16_) | copy-start | bytes 589828
  18.8 1.6 %copy-start.9 = (f32[1,128,4096]{2,1,0:T(8,128)S(1)}, f32[1,128,4096]{2,1,0:T(8,128)}, u32[]{:S(2)}) copy-start(f32[1,128,4096]{2,1,0:T(8,128)} %param.18) | copy-start | bytes 6291460
  20.4 0.8 %copy-start.15 = (bf16[128,256]{1,0:T(8,128)(2,1)S(1)}, bf16[128,256]{1,0:T(8,128)(2,1)}, u32[]{:S(2)}) copy-start(bf16[128,256]{1,0:T(8,128)(2,1)} %constant.66.clone.refs_7_.refs_10_) | copy-start | bytes 196612
  21.2 1.4 %copy-start.10 = (f32[384,128]{1,0:T(8,128)S(1)}, f32[384,128]{1,0:T(8,128)}, u32[]{:S(2)}) copy-start(f32[384,128]{1,0:T(8,128)} %constant.60.clone.refs_7_) | copy-start | bytes 589828
  21.2 1.4 %copy-start.13 = (bf16[384,128]{1,0:T(8,128)(2,1)S(1)}, bf16[384,128]{1,0:T(8,128)(2,1)}, u32[]{:S(2)}) copy-start(bf16[384,128]{1,0:T(8,128)(2,1)} %constant.62.clone.refs_9_) | copy-start | bytes 294916
  21.2 1.4 %copy-start.17 = (bf16[64,192]{1,0:T(8,128)(2,1)S(1)}, bf16[64,192]{1,0:T(8,128)(2,1)}, u32[]{:S(2)}) copy-start(bf16[64,192]{1,0:T(8,128)(2,1)} %constant.61.clone.refs_8_) | copy-start | bytes 73732
  21.2 1.4 %copy-start.20 = (f32[8,128]{1,0:T(8,128)S(1)}, f32[8,128]{1,0:T(8,128)}, u32[]{:S(2)}) copy-start(f32[8,128]{1,0:T(8,128)} %constant.68.clone.refs_12_) | copy-start | bytes 12292
  21.2 1.4 %copy-start.22 = (s32[2,6]{1,0:T(2,128)S(1)}, s32[2,6]{1,0:T(2,128)}, u32[]{:S(2)}) copy-start(s32[2,6]{1,0:T(2,128)} %listed.7) | copy-start | bytes 148
  21.3 11.1 %copy-start.2 = (f32[128,4096]{1,0:T(8,128)S(1)}, f32[128,4096]{1,0:T(8,128)}, u32[]{:S(2)}) copy-start(f32[128,4096]{1,0:T(8,128)} %constant.57.clone.refs_4_.refs_14_) | copy-start | bytes 6291460
  21.3 11.1 %copy-start.4 = (f32[128,4096]{1,0:T(8,128)S(1)}, f32[128,4096]{1,0:T(8,128)}, u32[]{:S(2)}) copy-start(f32[128,4096]{1,0:T(8,128)} %constant.56.clone.refs_2_.refs_3_) | copy-start | bytes 6291460
  21.3 11.1 %copy-start.16 = (bf16[128,32]{1,0:T(8,128)(2,1)S(1)}, bf16[128,32]{1,0:T(8,128)(2,1)}, u32[]{:S(2)}) copy-start(bf16[128,32]{1,0:T(8,128)(2,1)} %constant.59.clone.refs_5_.refs_15_) | copy-start | bytes 24580
  24.4 4.7 %collective-permute-start.6 = (f32[96,128]{1,0:T(8,128)S(1)}, f32[96,128]{1,0:T(8,128)S(1)}, u32[]{:S(2)}, u32[]{:S(2)}) collective-permute-start(f32[96,128]{1,0:T(8,128)S(1)} %get-tuple-element.38), channel_id=1, source_target_pairs={{0,8},{1,4},{2,5},{3,6},{4,1},{5,2},{6,3},{7,15},{8,0},{9,12},{10,... | collective-permute-start | bytes 147464 | tf_op jit(solution)/shard_map/ppermute | solution.py:620
  24.9 9.9 %collective-permute-start.7 = (f32[96,128]{1,0:T(8,128)S(1)}, f32[96,128]{1,0:T(8,128)S(1)}, u32[]{:S(2)}, u32[]{:S(2)}) collective-permute-start(f32[96,128]{1,0:T(8,128)S(1)} %get-tuple-element.39), channel_id=1, source_target_pairs={{0,4},{1,5},{2,6},{3,7},{4,0},{5,1},{6,2},{7,3},{8,12},{9,13},{10,... | collective-permute-start | bytes 147464 | tf_op jit(solution)/shard_map/ppermute | solution.py:620
  25.0 9.8 %collective-permute-start.8 = (f32[96,128]{1,0:T(8,128)S(1)}, f32[96,128]{1,0:T(8,128)S(1)}, u32[]{:S(2)}, u32[]{:S(2)}) collective-permute-start(f32[96,128]{1,0:T(8,128)S(1)} %get-tuple-element.40), channel_id=1, source_target_pairs={{0,5},{1,6},{2,7},{3,11},{4,12},{5,0},{6,1},{7,2},{8,13},{9,14},{1... | collective-permute-start | bytes 147464 | tf_op jit(solution)/shard_map/ppermute | solution.py:620
  28.3 6.5 %collective-permute-start.9 = (f32[96,128]{1,0:T(8,128)S(1)}, f32[96,128]{1,0:T(8,128)S(1)}, u32[]{:S(2)}, u32[]{:S(2)}) collective-permute-start(f32[96,128]{1,0:T(8,128)S(1)} %get-tuple-element.41), channel_id=1, source_target_pairs={{0,29},{1,30},{2,31},{3,11},{4,12},{5,8},{6,9},{7,10},{8,5},{9,6},... | collective-permute-start | bytes 147464 | tf_op jit(solution)/shard_map/ppermute | solution.py:620
  28.3 6.5 %collective-permute-start.10 = (f32[96,128]{1,0:T(8,128)S(1)}, f32[96,128]{1,0:T(8,128)S(1)}, u32[]{:S(2)}, u32[]{:S(2)}) collective-permute-start(f32[96,128]{1,0:T(8,128)S(1)} %get-tuple-element.42), channel_id=1, source_target_pairs={{0,28},{1,29},{2,30},{3,31},{4,8},{5,9},{6,10},{7,11},{8,4},{9,5},... | collective-permute-start | bytes 147464 | tf_op jit(solution)/shard_map/ppermute | solution.py:620
  29.1 5.7 %collective-permute-start.11 = (f32[96,128]{1,0:T(8,128)S(1)}, f32[96,128]{1,0:T(8,128)S(1)}, u32[]{:S(2)}, u32[]{:S(2)}) collective-permute-start(f32[96,128]{1,0:T(8,128)S(1)} %get-tuple-element.43), channel_id=1, source_target_pairs={{0,1},{1,0},{2,29},{3,30},{4,9},{5,10},{6,11},{7,15},{8,16},{9,4},... | collective-permute-start | bytes 147464 | tf_op jit(solution)/shard_map/ppermute | solution.py:620
  36.6 4.8 %collective-permute-start.12 = (f32[96,128]{1,0:T(8,128)S(1)}, f32[96,128]{1,0:T(8,128)S(1)}, u32[]{:S(2)}, u32[]{:S(2)}) collective-permute-start(f32[96,128]{1,0:T(8,128)S(1)} %get-tuple-element.47), channel_id=1, source_target_pairs={{0,8},{1,4},{2,5},{3,6},{4,1},{5,2},{6,3},{7,15},{8,0},{9,12},{10,... | collective-permute-start | bytes 147464 | tf_op jit(solution)/shard_map/ppermute | solution.py:620
  36.7 11.9 %collective-permute-start.13 = (f32[96,128]{1,0:T(8,128)S(1)}, f32[96,128]{1,0:T(8,128)S(1)}, u32[]{:S(2)}, u32[]{:S(2)}) collective-permute-start(f32[96,128]{1,0:T(8,128)S(1)} %get-tuple-element.48), channel_id=1, source_target_pairs={{0,4},{1,5},{2,6},{3,7},{4,0},{5,1},{6,2},{7,3},{8,12},{9,13},{10,... | collective-permute-start | bytes 147464 | tf_op jit(solution)/shard_map/ppermute | solution.py:620
  38.4 10.2 %collective-permute-start.14 = (f32[96,128]{1,0:T(8,128)S(1)}, f32[96,128]{1,0:T(8,128)S(1)}, u32[]{:S(2)}, u32[]{:S(2)}) collective-permute-start(f32[96,128]{1,0:T(8,128)S(1)} %get-tuple-element.49), channel_id=1, source_target_pairs={{0,5},{1,6},{2,7},{3,11},{4,12},{5,0},{6,1},{7,2},{8,13},{9,14},{1... | collective-permute-start | bytes 147464 | tf_op jit(solution)/shard_map/ppermute | solution.py:620
  40.8 7.8 %collective-permute-start.15 = (f32[96,128]{1,0:T(8,128)S(1)}, f32[96,128]{1,0:T(8,128)S(1)}, u32[]{:S(2)}, u32[]{:S(2)}) collective-permute-start(f32[96,128]{1,0:T(8,128)S(1)} %get-tuple-element.50), channel_id=1, source_target_pairs={{0,29},{1,30},{2,31},{3,11},{4,12},{5,8},{6,9},{7,10},{8,5},{9,6},... | collective-permute-start | bytes 147464 | tf_op jit(solution)/shard_map/ppermute | solution.py:620
  40.8 7.8 %collective-permute-start.16 = (f32[96,128]{1,0:T(8,128)S(1)}, f32[96,128]{1,0:T(8,128)S(1)}, u32[]{:S(2)}, u32[]{:S(2)}) collective-permute-start(f32[96,128]{1,0:T(8,128)S(1)} %get-tuple-element.51), channel_id=1, source_target_pairs={{0,28},{1,29},{2,30},{3,31},{4,8},{5,9},{6,10},{7,11},{8,4},{9,5},... | collective-permute-start | bytes 147464 | tf_op jit(solution)/shard_map/ppermute | solution.py:620
  41.4 7.3 %collective-permute-start.17 = (f32[96,128]{1,0:T(8,128)S(1)}, f32[96,128]{1,0:T(8,128)S(1)}, u32[]{:S(2)}, u32[]{:S(2)}) collective-permute-start(f32[96,128]{1,0:T(8,128)S(1)} %get-tuple-element.52), channel_id=1, source_target_pairs={{0,1},{1,0},{2,29},{3,30},{4,9},{5,10},{6,11},{7,15},{8,16},{9,4},... | collective-permute-start | bytes 147464 | tf_op jit(solution)/shard_map/ppermute | solution.py:620
  45.0 3.7 %copy-start.8 = (f32[384,128]{1,0:T(8,128)S(1)}, f32[384,128]{1,0:T(8,128)}, u32[]{:S(2)}) copy-start(f32[384,128]{1,0:T(8,128)} %constant.65.clone.refs_6_.refs_9_.refs_16_) | copy-start | bytes 589828
where the time goes:
time: 53.1 us; the launch traced here: 52.8 us
  starting transfers between devices  24.1 us (45%)
  Pallas kernels  15.9 us (30%)
  local copies, waits for them, and re-layouts  10.4 us (20%)
  between operations  1.62 us (3%)
  waiting for transfers between devices  0.75 us (1%)
    ppermute x18, starting transfers between devices, exchange(): arrived[i] = lax.ppermute(payloads[i], ('gx', 'gy'), routes[i])  24.1 us
    pallas_call x7, Pallas kernels, run(): pl.pallas_call(body, out_shape=[jax.ShapeDtypeStruct(s, jnp.float32) for...  15.9 us
    unnamed x47, local copies, waits for them, and re-layouts  10.4 us
  transfers between devices with their start and end apart: 18, of which 1 were waited for; matrix products, arithmetic and copies ran while one was open for 0% of the time, Pallas kernels for 14%

commit v1 on v0

--- a/solution.py
+++ b/solution.py
@@ -132,6 +132,38 @@
     return [(x * ny + y, u * ny + v) for (x, y), (u, v) in sorted(taken.items())]
 
 
+def noted(card):
+    bits = card[1][0]
+    return card[0][0] > 0, bits & 1 == 1, [bits & (2 << i) != 0 for i in range(len(SHIFTS))]
+
+
+def position(shape, along, across):
+    bits = 1 - along % 2
+    for i, g in enumerate(SHIFTS):
+        met = (along > 0) & (across - g >= 0) & (across - g < shape[1])
+        bits = bits + jnp.where(met, 2 << i, 0)
+    return bits
+
+
+def folded(step, one, two, live):
+    return (step + 1) + ((one + OFF) << 2) + ((two + OFF) << 8) + (jnp.where(live, 1, 0) << 14)
+
+
+def joints(rows_folded, count):
+    rows = []
+    for n in range(count):
+        bits = rows_folded[n, 0]
+        rows.append(
+            (
+                (bits & 3) - 1,
+                ((bits >> 2) & 63) - OFF,
+                ((bits >> 8) & 63) - OFF,
+                (bits >> 14) & 1 == 1,
+            )
+        )
+    return rows
+
+
 def left_lanes(shape):
     return lax.broadcasted_iota(jnp.int32, shape, len(shape) - 1) < shape[-1] // 2
 
@@ -196,7 +228,7 @@
     ]
 
 
-def emit_payloads(layers, listed, place, outs, pads):
+def emit_payloads(layers, even, listed, outs, pads):
     side = layers.shape[0] // 3
     half = side // 2
     wide = layers.shape[1]
@@ -208,22 +240,20 @@
     for r, plane in enumerate(blended(planes)):
         pads[0, r, OFF : OFF + side] = jnp.where(whole, turned(plane), 0.0)
     packed = []
-    for s in range(listed.shape[0]):
-        start = OFF + listed[s, 3]
-        roll = (wide - listed[s, 4]) % wide
-        opposite = (wide + half * 2 - listed[s, 4]) % wide
+    for _, one, two, _ in listed:
+        start = OFF + one
+        roll = (wide - two) % wide
+        opposite = (wide + side - two) % wide
         parts = []
         for r in range(3):
             top = pltpu.roll(pads[0, r, pl.ds(start, half)], roll, 1)
             bottom = pltpu.roll(pads[0, r, pl.ds(start + half, half)], opposite, 1)
             parts.append(jnp.where(left, top, bottom))
         packed.append(jnp.concatenate(parts, axis=0))
-    even = place[0] == 1
     for i, g in enumerate(SHIFTS):
         force = jnp.zeros_like(low)
-        for s in range(listed.shape[0]):
-            wanted = (listed[s, 2] == g) & (listed[s, 5] != 0)
-            force = force + jnp.where(wanted, packed[s], 0.0)
+        for part, (step, _, _, live) in zip(packed, listed):
+            force = force + jnp.where((step == g) & live, part, 0.0)
         outs[i][...] = jnp.where(even, force, low)
         outs[3 + i][...] = jnp.where(even, low, force)
 
@@ -237,28 +267,26 @@
             pads[n, r, OFF + side : 2 * OFF + side] = blank
 
 
-def take_forces(arrived, listed, place, pads):
+def take_forces(arrived, even, met, listed, pads):
     wide = arrived[0].shape[1]
     half = arrived[0].shape[0] // 3
     side = 2 * half
     left = left_lanes((half, wide))
-    even = place[0] == 1
     lows = [jnp.where(even, arrived[i][...], arrived[3 + i][...]) for i in range(3)]
     pushes = [jnp.where(even, arrived[3 + i][...], arrived[i][...]) for i in range(3)]
     pushed = jnp.zeros_like(lows[0])
     for i in range(3):
-        pushed = pushed + jnp.where(place[1 + i] == 1, pushes[i], 0.0)
+        pushed = pushed + jnp.where(met[i], pushes[i], 0.0)
     high = [None] * 3
-    for s in range(listed.shape[0]):
-        g = listed[s, 2]
+    for s, (g, one, two, live) in enumerate(listed):
         chosen = jnp.where(g == 0, lows[1], jnp.where(g < 0, lows[0], lows[2]))
-        chosen = jnp.where(listed[s, 5] != 0, chosen, 0.0)
+        chosen = jnp.where(live, chosen, 0.0)
         for r in range(3):
             part = chosen[r * half : (r + 1) * half]
             pads[1 + s, r, OFF : OFF + half] = jnp.where(left, part, 0.0)
             pads[1 + s, r, OFF + half : OFF + side] = jnp.where(left, turned(part), 0.0)
-        start = OFF - listed[s, 3]
-        roll = (listed[s, 4] + wide + side) % wide
+        start = OFF - one
+        roll = (two + wide + side) % wide
         for r in range(3):
             moved = pltpu.roll(pads[1 + s, r, pl.ds(start, side)], roll, 1)
             high[r] = moved if high[r] is None else high[r] + moved
@@ -444,157 +472,251 @@
     return sums + jnp.concatenate(across, axis=1)
 
 
-def start_kernel(flag, listed, place, state, collect, inverse_one, inverse_two, *rest):
-    outs, (layers, pads, gathered, woven) = rest[:6], rest[6:]
+def copies(pairs, sems, first=0):
+    return [
+        pltpu.make_async_copy(source, target, sems.at[first + i])
+        for i, (source, target) in enumerate(pairs)
+    ]
+
+
+def strips(ref, width=CHUNK):
+    return [slice(column, column + width) for column in range(0, ref.shape[-1], width)]
+
+
+def start_kernel(flags, place, listed, now, before, cosine, *refs):
+    sources, outs, folds, refs = refs[:3], refs[3:9], refs[9], refs[10:]
+    held, prior, factor, layers, pads, gathered, woven, rows, sems = refs[:9]
+    collect, inverse_one, inverse_two = refs[9:]
+    s0, total = held.shape
+    tiles = total // 128
+    spans = strips(held, 2 * CHUNK)
+    first = copies([(listed, rows)], sems)
+    tables = copies(zip(sources, (collect, inverse_one, inverse_two)), sems, 1)
+    moves = copies([(now.at[0, :, p], held.at[:, p]) for p in spans], sems, 4)
+    past = copies([(before.at[0], prior)], sems, 4 + len(spans))[0]
+    more = copies([(cosine, factor)], sems, 5 + len(spans))[0]
+    for m in tables[:1] + moves + tables[1:] + first:
+        m.start()
     clear_pads(pads)
+    for m in moves[: len(moves) // 2]:
+        m.wait()
+    past.start()
+    _, even, _ = noted((flags, place))
+    first[0].wait()
+    entries = []
+    for n in range(listed.shape[0]):
+        entries.append((rows[n, 2], rows[n, 3], rows[n, 4], rows[n, 5] != 0))
+        folds[n : n + 1, :] = jnp.full((1, 128), folded(*entries[n]), jnp.int32)
+
+    for m in tables:
+        m.wait()
+
+    @pl.when(flags[0] > 0)
+    def _():
+        for m in moves[len(moves) // 2 :]:
+            m.wait()
+        layers[...] = pml_planes(held, gathered, woven)
+
+    @pl.when(flags[0] <= 0)
+    def _():
+        more.start()
+        for i, p in enumerate(spans):
+            if i >= len(moves) // 2:
+                moves[i].wait()
+            scatter_tiles(collected(held[:, p], collect), gathered.at[0 : 8 * tiles], p.start)
+        modes = planes_of_modes(gathered, tiles)
+        layers[...] = mirrored_inverse(modes, inverse_one, inverse_two)
+
+    emit_payloads(layers[...], even, entries, outs, pads)
+
+    past.wait()
+
+    @pl.when(flags[0] <= 0)
+    def _():
+        more.wait()
+
+
+def free_kernel(pushed, flag, *refs):
+    if pushed:
+        forces, _, before, cosine, gain, inject = refs[:6]
+        refs = refs[6:]
+        collect, inverse_one, inverse_two, rows, down, inside, whole = refs[:7]
+    else:
+        whole, before, cosine, collect, inverse_one, inverse_two, rows = refs[:7]
+        down, inside = refs[7:9]
+        refs = refs[2:]
+    free, layers, gathered, woven = refs[7:]
+    s0, total = free.shape
+    tiles = total // 128
 
     @pl.when(flag[0] > 0)
     def _():
-        layers[...] = pml_planes(state, gathered, woven)
-
-    @pl.when(flag[0] <= 0)
-    def _():
-        for column in range(0, state.shape[1], CHUNK):
-            rows = collected(state[:, column : column + CHUNK], collect)
-            scatter_tiles(rows, gathered.at[0 : 8 * tile_count(state)], column)
-        modes = planes_of_modes(gathered, tile_count(state))
-        layers[...] = mirrored_inverse(modes, inverse_one, inverse_two)
-
-    emit_payloads(layers[...], listed, place, outs, pads)
-
-
-def free_kernel(first, keep, flag, *refs):
-    refs = list(refs)
-    forces = None if first else refs.pop(0)
-    current, before, cosine = refs[:3]
-    refs = refs[3:]
-    gain, inject = (None, None) if first else (refs.pop(0), refs.pop(0))
-    collect, inverse_one, inverse_two, rows, down, inside = refs[:6]
-    refs = refs[6:]
-    whole = refs.pop(0) if keep else current
-    free, layers, gathered, woven = refs
-    s0, total = current.shape
-    tiles = total // 128
-
-    @pl.when(flag[0] > 0)
-    def _():
-        if keep:
+        if pushed:
             spread_pml_forces(forces[...], gathered, woven)
-            for column in range(0, total, CHUNK):
-                span = slice(column, column + CHUNK)
-                whole[8 : s0 - 8, span] = current[8 : s0 - 8, span]
-                for at, base in ((0, 0), (s0 - 8, 8)):
-                    scale = wide(rows[2 * s0 + at : 2 * s0 + at + 8, :], CHUNK)
-                    whole[at : at + 8, span] = current[at : at + 8, span] + scale * pml_rows(
-                        gathered, column, CHUNK, base
-                    )
-        for column in range(0, total, CHUNK):
-            span = slice(column, column + CHUNK)
-            sums = stencil_sums(whole, column, CHUNK, down, inside)
-            free[:, span] = (
-                wide(rows[0:s0, :], CHUNK) * whole[:, span]
-                + wide(rows[s0 : 2 * s0, :], CHUNK) * before[:, span]
+        for p in strips(free) if pushed else ():
+            for at, base in ((0, 0), (s0 - 8, 8)):
+                scale = wide(rows[2 * s0 + at : 2 * s0 + at + 8, :], CHUNK)
+                whole[at : at + 8, p] = whole[at : at + 8, p] + scale * pml_rows(
+                    gathered, p.start, CHUNK, base
+                )
+        for p in strips(free):
+            sums = stencil_sums(whole, p.start, CHUNK, down, inside)
+            free[:, p] = (
+                wide(rows[0:s0, :], CHUNK) * whole[:, p]
+                + wide(rows[s0 : 2 * s0, :], CHUNK) * before[:, p]
                 + wide(rows[2 * s0 : 3 * s0, :], CHUNK) * (sums * (1.0 / 180.0))
             )
         layers[...] = pml_planes(free, gathered, woven)
 
     @pl.when(flag[0] <= 0)
     def _():
-        if keep:
+        if pushed:
             spread_modal_forces(forces[...], gathered)
         parts = []
-        for column in range(0, total, CHUNK):
-            span = slice(column, column + CHUNK)
-            value = current[:, span]
-            if keep:
-                value = value + gain[:, span] * injected(gathered, inject, column, CHUNK)
-                whole[:, span] = value
-            value = cosine[:, span] * value - before[:, span]
-            free[:, span] = value
+        for p in strips(free):
+            value = whole[:, p]
+            if pushed:
+                value = value + gain[:, p] * injected(gathered, inject, p.start, CHUNK)
+                whole[:, p] = value
+            value = cosine[:, p] * value - before[:, p]
+            free[:, p] = value
             parts.append(collected(value, collect))
         for i, part in enumerate(parts):
             scatter_tiles(part, gathered.at[0 : 8 * tiles], i * CHUNK)
         layers[...] = mirrored_inverse(planes_of_modes(gathered, tiles), inverse_one, inverse_two)
 
 
-def advance_layers(flag, listed, place, arrived, layers, tables, forces, next_layers, pads):
-    coupled, forward_one, forward_two, inverse_one, inverse_two, face_third = tables
+def face_forces(card, folds, arrived, tables, forces, pads):
     clear_pads(pads)
-    push = take_forces(arrived, listed, place, pads)
-    side = push.shape[0] // 3
-
-    @pl.when(flag[0] > 0)
+    _, even, met = noted(card)
+    push = take_forces(arrived, even, met, joints(folds, pads.shape[0] - 1), pads)
+
+    @pl.when(noted(card)[0])
     def _():
         forces[...] = push
+
+    @pl.when(jnp.logical_not(noted(card)[0]))
+    def _():
+        forces[...] = mirrored_forward(push, tables[1], tables[2])
+
+
+def advance_layers(card, layers, tables, forces, next_layers):
+    coupled, _, _, inverse_one, inverse_two, face_third = tables
+    side = layers.shape[0] // 3
+
+    @pl.when(noted(card)[0])
+    def _():
         for r in range(3):
             span = slice(r * side, (r + 1) * side)
-            next_layers[span, :] = layers[span, :] + face_third[r : r + 1, :] * push[span]
-
-    @pl.when(flag[0] <= 0)
-    def _():
-        modes = mirrored_forward(push, forward_one, forward_two)
-        forces[...] = modes
-        answer = mirrored_inverse(modal_response(modes, coupled), inverse_one, inverse_two)
+            next_layers[span, :] = layers[span, :] + face_third[r : r + 1, :] * forces[span, :]
+
+    @pl.when(jnp.logical_not(noted(card)[0]))
+    def _():
+        answer = mirrored_inverse(modal_response(forces[...], coupled), inverse_one, inverse_two)
         next_layers[...] = layers[...] + answer
 
 
-def force_kernel(flag, listed, place, *refs):
+def force_kernel(*refs):
+    card, folds, refs = refs[:2], refs[2], refs[3:]
     arrived, layers, tables = refs[:6], refs[6], refs[7:13]
     forces, outs, (next_layers, pads) = refs[13], refs[14:20], refs[20:]
-    advance_layers(flag, listed, place, arrived, layers, tables, forces, next_layers, pads)
-    emit_payloads(next_layers[...], listed, place, outs, pads)
-
-
-def last_kernel(flag, listed, place, *refs):
+    face_forces(card, folds, arrived, tables, forces, pads)
+    advance_layers(card, layers, tables, forces, next_layers)
+    listed = joints(folds, pads.shape[0] - 1)
+    emit_payloads(next_layers[...], noted(card)[1], listed, outs, pads)
+
+
+def last_kernel(*refs):
+    card, folds, refs = refs[:2], refs[2], refs[3:]
     arrived, layers, tables = refs[:6], refs[6], refs[7:13]
     free, gain, inject, rows = refs[13:17]
-    state, faces, forces, next_layers, pads, gathered, woven = refs[17:]
-    advance_layers(flag, listed, place, arrived, layers, tables, forces, next_layers, pads)
+    state, faces, forces, next_layers, pads, gathered, woven, held, sems = refs[17:]
     s0, total = free.shape
     tiles = total // 128
-
-    @pl.when(flag[0] > 0)
+    spans = strips(free)
+    middle = slice(8, s0 - 8)
+    ends = ((0, 0), (s0 - 8, 8))
+    inner = copies([(free.at[middle], state.at[0, middle])], sems)
+    outer = copies(
+        [(held.at[at : at + 8], state.at[0, at : at + 8]) for at, _ in ends], sems, 1
+    )
+    moves = copies([(held.at[:, p], state.at[0, :, p]) for p in spans], sems)
+
+    @pl.when(noted(card)[0])
+    def _():
+        inner[0].start()
+
+    face_forces(card, folds, arrived, tables, forces, pads)
+
+    @pl.when(noted(card)[0])
     def _():
         spread_pml_forces(forces[...], gathered, woven)
-        state[8 : s0 - 8, :] = free[8 : s0 - 8, :]
-        for column in range(0, total, CHUNK):
-            span = slice(column, column + CHUNK)
-            for at, base in ((0, 0), (s0 - 8, 8)):
+        for p in spans:
+            for at, base in ends:
                 scale = wide(rows[2 * s0 + at : 2 * s0 + at + 8, :], CHUNK)
-                state[at : at + 8, span] = free[at : at + 8, span] + scale * pml_rows(
-                    gathered, column, CHUNK, base
+                held[at : at + 8, p] = free[at : at + 8, p] + scale * pml_rows(
+                    gathered, p.start, CHUNK, base
                 )
-
-    @pl.when(flag[0] <= 0)
+        for m in outer:
+            m.start()
+
+    @pl.when(jnp.logical_not(noted(card)[0]))
     def _():
         spread_modal_forces(forces[...], gathered)
-        for column in range(0, total, CHUNK):
-            span = slice(column, column + CHUNK)
-            state[:, span] = free[:, span] + gain[:, span] * injected(gathered, inject, column, CHUNK)
-
+        for m, p in zip(moves, spans):
+            held[:, p] = free[:, p] + gain[:, p] * injected(gathered, inject, p.start, CHUNK)
+            m.start()
+
+    advance_layers(card, layers, tables, forces, next_layers)
     shown = low_high_rows(next_layers[...], woven, tiles)
     for r in range(3):
         gathered[r * tiles : (r + 1) * tiles, :] = shown[r][0]
         gathered[(3 + r) * tiles : (4 + r) * tiles, :] = shown[r][1]
-    for J in range(tiles):
-        faces[:, J * 128 : (J + 1) * 128] = gathered[pl.ds(J, 8, stride=tiles), :][0:6]
+    last = pltpu.make_async_copy(gathered.at[0 : 6 * tiles], faces, sems.at[len(spans)])
+    last.start()
+
+    @pl.when(noted(card)[0])
+    def _():
+        for m in inner + outer:
+            m.wait()
+
+    @pl.when(jnp.logical_not(noted(card)[0]))
+    def _():
+        for m in moves:
+            m.wait()
+
+    last.wait()
 
 
 SCALAR = pl.BlockSpec(memory_space=pltpu.SMEM)
 BLOCK = pl.BlockSpec(memory_space=pltpu.VMEM)
-
-
-def run(body, scalars, blocks, outs, scratch, flops=0):
+FAR = pl.BlockSpec(memory_space=pltpu.HBM)
+
+
+def run(body, blocks, outs, scratch, near=(), far=(), far_outs=(), aliases=None, flops=0):
     moved = sum(b.size * b.dtype.itemsize for b in blocks)
+    blocks = [
+        pltpu.with_memory_space_constraint(b, pltpu.HBM) if i in far else b
+        for i, b in enumerate(blocks)
+    ]
+    spots = {**dict.fromkeys(far, FAR), **dict.fromkeys(near, SCALAR)}
     return pl.pallas_call(
         body,
-        out_shape=[jax.ShapeDtypeStruct(s, jnp.float32) for s in outs],
-        in_specs=[SCALAR] * len(scalars) + [BLOCK] * len(blocks),
-        out_specs=[BLOCK] * len(outs),
-        scratch_shapes=[pltpu.VMEM(s, jnp.float32) for s in scratch],
+        out_shape=[
+            jax.ShapeDtypeStruct(s, jnp.float32) if isinstance(s, tuple) else s for s in outs
+        ],
+        in_specs=[spots.get(i, BLOCK) for i in range(len(blocks))],
+        out_specs=[
+            FAR if i in far_outs else BLOCK
+            for i, s in enumerate(outs)
+        ],
+        scratch_shapes=[
+            pltpu.VMEM(s, jnp.float32) if isinstance(s, tuple) else s for s in scratch
+        ],
+        input_output_aliases=aliases or {},
         compiler_params=pltpu.CompilerParams(vmem_limit_bytes=32 * 1024 * 1024),
         cost_estimate=pl.CostEstimate(flops=flops, bytes_accessed=moved, transcendentals=0),
-    )(*scalars, *blocks)
+    )(*blocks)
 
 
 def local(nx, ny, state_now, state_prev, pml_flags, interfaces):
@@ -602,77 +724,77 @@
     side = math.isqrt(cross)
     t = {k: jnp.asarray(v) for k, v in make_tables(s0, side).items()}
     tiles = cross // 128
-    now, before = state_now[0], state_prev[0]
-    gx, gy = lax.axis_index("gx"), lax.axis_index("gy")
-    reach = [(gx > 0) & (gy - g >= 0) & (gy - g < ny) for g in SHIFTS]
-    place = jnp.stack([gx % 2 == 0, *reach]).astype(jnp.int32)
-    scalars = (pml_flags, interfaces, place)
     planes = (3 * side, 128)
     packed = (3 * side // 2, 128)
     pads = (1 + interfaces.shape[0], 3, side + 2 * OFF, 128)
     gathered = (16 * tiles, 128)
+    full = (s0, cross)
+    count = cross // CHUNK
+    place = position((nx, ny), lax.axis_index("gx"), lax.axis_index("gy")).reshape(1)
+    card = (pml_flags, place)
     routes = [pairing(nx, ny, parity, g) for parity in (0, 1) for g in SHIFTS]
-    send_order = (5, 3, 4, 2, 0, 1)
 
     def exchange(payloads):
-        arrived = [None] * 6
-        for i in send_order:
-            arrived[i] = lax.ppermute(payloads[i], ("gx", "gy"), routes[i])
-        return arrived
-
-    payloads = run(
+        return [lax.ppermute(payloads[i], ("gx", "gy"), routes[i]) for i in range(6)]
+
+    result = run(
         start_kernel,
-        scalars,
-        (now, t["collect"], t["inverse_one"], t["inverse_two"]),
-        [packed] * 6,
-        [planes, pads, gathered, planes],
-    )
-    tables = [
-        t[k]
-        for k in ("coupled", "forward_one", "forward_two", "inverse_one", "inverse_two", "face_third")
-    ]
+        (
+            *(pml_flags, place, interfaces, state_now, state_prev, t["cosine"]),
+            *(t["collect"], t["inverse_one"], t["inverse_two"]),
+        ),
+        [packed] * 6 + [jax.ShapeDtypeStruct((8, 128), jnp.int32)] + [full] * 3,
+        [
+            *(planes, pads, gathered, planes),
+            pltpu.SMEM(interfaces.shape, jnp.int32),
+            pltpu.SemaphoreType.DMA((9 + count,)),
+            *(pltpu.VMEM(t[k].shape, t[k].dtype) for k in ("collect", "inverse_one", "inverse_two")),
+        ],
+        near=(0, 1),
+        far=range(2, 9),
+    )
+    payloads, (folds, now, before, cosine) = result[:6], result[6:]
+    names = ("coupled", "forward_one", "forward_two", "inverse_one", "inverse_two", "face_third")
+    tables = [t[k] for k in names]
     shared = [t[k] for k in ("collect", "inverse_one", "inverse_two", "rows", "down", "inside")]
-    forces = None
-    current = now
     for step in range(STEPS):
         arrived = exchange(payloads)
-        full = (s0, cross)
         if step == 0:
             free, layers = run(
-                functools.partial(free_kernel, True, False),
-                scalars[:1],
-                (current, before, t["cosine"], *shared),
+                functools.partial(free_kernel, False),
+                (pml_flags, now, before, cosine, *shared),
                 [full, planes],
                 [gathered, planes],
+                near=(0,),
                 flops=10**9,
             )
         else:
-            whole, free, layers = run(
-                functools.partial(free_kernel, False, True),
-                scalars[:1],
-                (forces, free, current, t["cosine"], t["gain"], t["inject"], *shared),
+            now, free, layers = run(
+                functools.partial(free_kernel, True),
+                (pml_flags, forces, free, now, cosine, t["gain"], t["inject"], *shared),
                 [full, full, planes],
                 [gathered, planes],
+                near=(0,),
+                aliases={2: 0},
                 flops=10**9,
             )
-            current = whole
         if step < STEPS - 1:
             forces, *payloads = run(
                 force_kernel,
-                scalars,
-                (*arrived, layers, *tables),
+                (*card, folds, *arrived, layers, *tables),
                 [planes] + [packed] * 6,
                 [planes, pads],
+                near=(0, 1),
             )
-        else:
-            state, faces = run(
-                last_kernel,
-                scalars,
-                (*arrived, layers, *tables, free, t["gain"], t["inject"], t["rows"]),
-                [full, (6, cross)],
-                [planes, planes, pads, gathered, planes],
-            )
-    return state[None], faces[None]
+    state, faces = run(
+        last_kernel,
+        (*card, folds, *arrived, layers, *tables, free, t["gain"], t["inject"], t["rows"]),
+        [(1, s0, cross), (6 * tiles, 128)],
+        [*(planes, planes, pads, gathered, planes, full), pltpu.SemaphoreType.DMA((3 + count,))],
+        near=(0, 1),
+        far_outs=(0, 1),
+    )
+    return state, faces.reshape(1, 6, cross)
 
 
 def solution(mesh):

time: 53.1 us -> 42.8 us (0.81)
  local copies, waits for them, and re-layouts: 10.4 us -> 0.08 us
  Pallas kernels: 15.9 us -> 14.7 us
  waiting for transfers between devices: 0.75 us -> 1.55 us
    unnamed x47 -> x24, local copies, waits for them, and re-layouts: 10.4 us -> 0.08 us
    pallas_call x7, Pallas kernels: 15.9 us -> 14.7 us  [run(): pl.pallas_call(body, out_shape=[jax.ShapeDtypeStruct(s, jnp.float32) if i...]
    ppermute x18, waiting for transfers between devices: 0.75 us -> 1.55 us  [exchange(): lax.ppermute(payloads[i], ('gx', 'gy'), routes[i])]
    ppermute x18, starting transfers between devices: 24.1 us -> 24.6 us  [exchange(): lax.ppermute(payloads[i], ('gx', 'gy'), routes[i])]
  transfers between devices with their start and end apart: 18 -> 18, of which waited for: 1 -> 2; matrix products, arithmetic and copies ran while one was open for 0% -> 0% of each run, Pallas kernels for 14% -> 14%
where the time goes in v1:
time: 42.8 us; the launch traced here: 42.7 us
  starting transfers between devices  24.6 us (57%)
  Pallas kernels  14.7 us (34%)
  between operations  1.76 us (4%)
  waiting for transfers between devices  1.55 us (4%)
    ppermute x18, starting transfers between devices, exchange(): lax.ppermute(payloads[i], ('gx', 'gy'), routes[i])  24.6 us
    pallas_call x7, Pallas kernels, run(): pl.pallas_call(body, out_shape=[jax.ShapeDtypeStruct(s, jnp.float32) if i...  14.7 us
    ppermute x18, waiting for transfers between devices, exchange(): lax.ppermute(payloads[i], ('gx', 'gy'), routes[i])  1.55 us
  transfers between devices with their start and end apart: 18, of which 2 were waited for; matrix products, arithmetic and copies ran while one was open for 0% of the time, Pallas kernels for 14%

profile of v1, /device:TPU:0, one launch (start us, length us, event | category | flops | bytes accessed | tf_op | source)
XLA Modules:
  0.0 42.7 jit_solution(16974648880030756985)
XLA Ops:
  1.3 0.0 copy-start.1
  1.3 0.0 copy-start.2
  1.3 0.0 copy-start.4
  1.3 0.0 copy-start.6
  1.4 0.0 copy-start.7
  1.4 0.0 copy-start.10
  1.4 3.8 %shard_map.176 = (f32[96,128]{1,0:T(8,128)S(1)}, f32[96,128]{1,0:T(8,128)S(1)}, f32[96,128]{1,0:T(8,128)S(1)}, f32[96,128]{1,0:T(8,128)S(1)}, f32[96,128]{1,0:T(...) custom-call(s32[1]{0:T(128)S(6)} %copy.25.flags.flag.refs_0_, ...), custom_call_target="tpu_custom_call" | custom-call | bytes 6422584 | tf_op jit(solution)/shard_map/pallas_call | solution.py:703
  5.2 3.0 %collective-permute-start = (f32[96,128]{1,0:T(8,128)S(1)}, f32[96,128]{1,0:T(8,128)S(1)}, u32[]{:S(2)}, u32[]{:S(2)}) collective-permute-start(f32[96,128]{1,0:T(8,128)S(1)} %get-tuple-element.36), channel_id=1, source_target_pairs={{0,8},{1,4},{2,5},{3,6},{4,1},{5,2},{6,3},{7,15},{8,0},{9,12},{10,... | collective-permute-start | bytes 147464 | tf_op jit(solution)/shard_map/ppermute | solution.py:738
  8.2 0.2 collective-permute-start.1
  8.4 1.2 %collective-permute-start.2 = (f32[96,128]{1,0:T(8,128)S(1)}, f32[96,128]{1,0:T(8,128)S(1)}, u32[]{:S(2)}, u32[]{:S(2)}) collective-permute-start(f32[96,128]{1,0:T(8,128)S(1)} %get-tuple-element.38), channel_id=1, source_target_pairs={{0,5},{1,6},{2,7},{3,11},{4,12},{5,0},{6,1},{7,2},{8,13},{9,14},{1... | collective-permute-start | bytes 147464 | tf_op jit(solution)/shard_map/ppermute | solution.py:738
  9.6 2.4 %collective-permute-start.3 = (f32[96,128]{1,0:T(8,128)S(1)}, f32[96,128]{1,0:T(8,128)S(1)}, u32[]{:S(2)}, u32[]{:S(2)}) collective-permute-start(f32[96,128]{1,0:T(8,128)S(1)} %get-tuple-element.39), channel_id=1, source_target_pairs={{0,29},{1,30},{2,31},{3,11},{4,12},{5,8},{6,9},{7,10},{8,5},{9,6},... | collective-permute-start | bytes 147464 | tf_op jit(solution)/shard_map/ppermute | solution.py:738
  12.0 0.0 collective-permute-start.4
  12.0 0.0 collective-permute-done.refs_3_
  12.0 1.7 %collective-permute-start.5 = (f32[96,128]{1,0:T(8,128)S(1)}, f32[96,128]{1,0:T(8,128)S(1)}, u32[]{:S(2)}, u32[]{:S(2)}) collective-permute-start(f32[96,128]{1,0:T(8,128)S(1)} %get-tuple-element.41), channel_id=1, source_target_pairs={{0,1},{1,0},{2,29},{3,30},{4,9},{5,10},{6,11},{7,15},{8,16},{9,4},... | collective-permute-start | bytes 147464 | tf_op jit(solution)/shard_map/ppermute | solution.py:738
  13.7 0.0 copy-start.3
  13.7 0.0 copy-start.5
  13.7 0.0 copy-start.9
  13.7 0.0 copy-start.11
  13.8 0.0 copy-start
  13.8 0.0 copy-start.8
  13.8 1.1 %shard_map.177 = (f32[128,4096]{1,0:T(8,128)S(1)}, f32[192,128]{1,0:T(8,128)S(1)}) custom-call(s32[1]{0:T(128)S(6)} %copy.25.flags.flag.refs_0_, f32[128,4096]{1,0:T(8,128)S(1)} %get-tuple-element.42.refs_0_.refs_2_, f32[128,4096]{1,0:T(8,128)S(1)} %get-tuple-element.43.refs_1_, f32[128,4096]{1,0:T(8,128)S(1)} %get-tuple-element.44.refs_2_.refs_3_, ...), custom_call_target="tpu_custom_call" | custom-call | flops 1000000000 | bytes 6750212 | tf_op jit(solution)/shard_map/pallas_call | solution.py:703
  14.9 0.0 collective-permute-done.1.refs_4_
  14.9 0.0 collective-permute-done.2.refs_5_
  14.9 0.1 collective-permute-done.3.refs_6_
  15.0 1.4 %collective-permute-done.4.refs_7_ = f32[96,128]{1,0:T(8,128)S(1)} collective-permute-done((f32[96,128]{1,0:T(8,128)S(1)}, f32[96,128]{1,0:T(8,128)S(1)}, u32[]{:S(2)}, u32[]{:S(2)}) %collective-permute-start.4) | collective-permute-done | bytes 49184 | tf_op jit(solution)/shard_map/ppermute | solution.py:738
  16.4 0.0 collective-permute-done.5.refs_8_
  16.4 1.3 %shard_map.178 = (f32[192,128]{1,0:T(8,128)S(1)}, f32[96,128]{1,0:T(8,128)S(1)}, f32[96,128]{1,0:T(8,128)S(1)}, f32[96,128]{1,0:T(8,128)S(1)}, f32[96,128]{1,0:T...) custom-call(s32[1]{0:T(128)S(6)} %copy.25.flags.flag.refs_0_, s32[1]{0:T(128)} %bitcast.place.refs_1_, ...), custom_call_target="tpu_custom_call" | custom-call | bytes 843784 | tf_op jit(solution)/shard_map/pallas_call | solution.py:703
  17.8 1.3 %collective-permute-start.6 = (f32[96,128]{1,0:T(8,128)S(1)}, f32[96,128]{1,0:T(8,128)S(1)}, u32[]{:S(2)}, u32[]{:S(2)}) collective-permute-start(f32[96,128]{1,0:T(8,128)S(1)} %get-tuple-element.46), channel_id=1, source_target_pairs={{0,8},{1,4},{2,5},{3,6},{4,1},{5,2},{6,3},{7,15},{8,0},{9,12},{10,... | collective-permute-start | bytes 147464 | tf_op jit(solution)/shard_map/ppermute | solution.py:738
  19.0 0.5 %collective-permute-start.7 = (f32[96,128]{1,0:T(8,128)S(1)}, f32[96,128]{1,0:T(8,128)S(1)}, u32[]{:S(2)}, u32[]{:S(2)}) collective-permute-start(f32[96,128]{1,0:T(8,128)S(1)} %get-tuple-element.47), channel_id=1, source_target_pairs={{0,4},{1,5},{2,6},{3,7},{4,0},{5,1},{6,2},{7,3},{8,12},{9,13},{10,... | collective-permute-start | bytes 147464 | tf_op jit(solution)/shard_map/ppermute | solution.py:738
  19.5 2.5 %collective-permute-start.8 = (f32[96,128]{1,0:T(8,128)S(1)}, f32[96,128]{1,0:T(8,128)S(1)}, u32[]{:S(2)}, u32[]{:S(2)}) collective-permute-start(f32[96,128]{1,0:T(8,128)S(1)} %get-tuple-element.48), channel_id=1, source_target_pairs={{0,5},{1,6},{2,7},{3,11},{4,12},{5,0},{6,1},{7,2},{8,13},{9,14},{1... | collective-permute-start | bytes 147464 | tf_op jit(solution)/shard_map/ppermute | solution.py:738
  22.1 0.3 collective-permute-start.9
  22.3 0.5 %collective-permute-start.10 = (f32[96,128]{1,0:T(8,128)S(1)}, f32[96,128]{1,0:T(8,128)S(1)}, u32[]{:S(2)}, u32[]{:S(2)}) collective-permute-start(f32[96,128]{1,0:T(8,128)S(1)} %get-tuple-element.50), channel_id=1, source_target_pairs={{0,28},{1,29},{2,30},{3,31},{4,8},{5,9},{6,10},{7,11},{8,4},{9,5},... | collective-permute-start | bytes 147464 | tf_op jit(solution)/shard_map/ppermute | solution.py:738
  22.9 3.3 %collective-permute-start.11 = (f32[96,128]{1,0:T(8,128)S(1)}, f32[96,128]{1,0:T(8,128)S(1)}, u32[]{:S(2)}, u32[]{:S(2)}) collective-permute-start(f32[96,128]{1,0:T(8,128)S(1)} %get-tuple-element.51), channel_id=1, source_target_pairs={{0,1},{1,0},{2,29},{3,30},{4,9},{5,10},{6,11},{7,15},{8,16},{9,4},... | collective-permute-start | bytes 147464 | tf_op jit(solution)/shard_map/ppermute | solution.py:738
  26.2 2.3 %shard_map.179 = (f32[128,4096]{1,0:T(8,128)S(1)}, f32[128,4096]{1,0:T(8,128)S(1)}, f32[192,128]{1,0:T(8,128)S(1)}) custom-call(s32[1]{0:T(128)S(6)} %copy.25.flags.flag.refs_0_, f32[192,128]{1,0:T(8,128)S(1)} %get-tuple-element.52.refs_0_, f32[128,4096]{1,0:T(8,128)S(1)} %get-tuple-element.53.refs_1_, ...), custom_call_target="tpu_custom_call", output_to_operand_aliasing={{0}: (2, {})} | custom-call | flops 1000000000 | bytes 8953860 | tf_op jit(solution)/shard_map/pallas_call | solution.py:703
  28.5 0.0 collective-permute-done.8.refs_5_
  28.5 0.0 collective-permute-done.9.refs_6_
  28.6 0.0 collective-permute-done.11.refs_8_
  28.6 1.3 %shard_map.180 = (f32[192,128]{1,0:T(8,128)S(1)}, f32[96,128]{1,0:T(8,128)S(1)}, f32[96,128]{1,0:T(8,128)S(1)}, f32[96,128]{1,0:T(8,128)S(1)}, f32[96,128]{1,0:T...) custom-call(s32[1]{0:T(128)S(6)} %copy.25.flags.flag.refs_0_, s32[1]{0:T(128)} %bitcast.place.refs_1_, ...), custom_call_target="tpu_custom_call" | custom-call | bytes 843784 | tf_op jit(solution)/shard_map/pallas_call | solution.py:703
  29.9 0.2 collective-permute-start.12
  30.1 1.7 %collective-permute-start.13 = (f32[96,128]{1,0:T(8,128)S(1)}, f32[96,128]{1,0:T(8,128)S(1)}, u32[]{:S(2)}, u32[]{:S(2)}) collective-permute-start(f32[96,128]{1,0:T(8,128)S(1)} %get-tuple-element.56), channel_id=1, source_target_pairs={{0,4},{1,5},{2,6},{3,7},{4,0},{5,1},{6,2},{7,3},{8,12},{9,13},{10,... | collective-permute-start | bytes 147464 | tf_op jit(solution)/shard_map/ppermute | solution.py:738
  31.7 1.8 %collective-permute-start.14 = (f32[96,128]{1,0:T(8,128)S(1)}, f32[96,128]{1,0:T(8,128)S(1)}, u32[]{:S(2)}, u32[]{:S(2)}) collective-permute-start(f32[96,128]{1,0:T(8,128)S(1)} %get-tuple-element.57), channel_id=1, source_target_pairs={{0,5},{1,6},{2,7},{3,11},{4,12},{5,0},{6,1},{7,2},{8,13},{9,14},{1... | collective-permute-start | bytes 147464 | tf_op jit(solution)/shard_map/ppermute | solution.py:738
  33.5 1.4 %collective-permute-start.16 = (f32[96,128]{1,0:T(8,128)S(1)}, f32[96,128]{1,0:T(8,128)S(1)}, u32[]{:S(2)}, u32[]{:S(2)}) collective-permute-start(f32[96,128]{1,0:T(8,128)S(1)} %get-tuple-element.59), channel_id=1, source_target_pairs={{0,28},{1,29},{2,30},{3,31},{4,8},{5,9},{6,10},{7,11},{8,4},{9,5},... | collective-permute-start | bytes 147464 | tf_op jit(solution)/shard_map/ppermute | solution.py:738
  34.9 0.0 collective-permute-done.12.refs_3_
  34.9 2.7 %collective-permute-start.17 = (f32[96,128]{1,0:T(8,128)S(1)}, f32[96,128]{1,0:T(8,128)S(1)}, u32[]{:S(2)}, u32[]{:S(2)}) collective-permute-start(f32[96,128]{1,0:T(8,128)S(1)} %get-tuple-element.60), channel_id=1, source_target_pairs={{0,1},{1,0},{2,29},{3,30},{4,9},{5,10},{6,11},{7,15},{8,16},{9,4},... | collective-permute-start | bytes 147464 | tf_op jit(solution)/shard_map/ppermute | solution.py:738
  37.6 2.3 %shard_map.181 = (f32[128,4096]{1,0:T(8,128)S(1)}, f32[128,4096]{1,0:T(8,128)S(1)}, f32[192,128]{1,0:T(8,128)S(1)}) custom-call(s32[1]{0:T(128)S(6)} %copy.25.flags.flag.refs_0_, f32[192,128]{1,0:T(8,128)S(1)} %get-tuple-element.61.refs_0_, f32[128,4096]{1,0:T(8,128)S(1)} %get-tuple-element.62.refs_1_, ...), custom_call_target="tpu_custom_call", output_to_operand_aliasing={{0}: (2, {})} | custom-call | flops 1000000000 | bytes 8953860 | tf_op jit(solution)/shard_map/pallas_call | solution.py:703
  40.0 0.0 collective-permute-done.14.refs_5_
  40.0 0.0 collective-permute-done.17.refs_8_
  40.0 2.5 %shard_map.182 = (f32[1,128,4096]{2,1,0:T(8,128)}, f32[192,128]{1,0:T(8,128)}) custom-call(s32[1]{0:T(128)S(6)} %copy.25.flags.flag.refs_0_, s32[1]{0:T(128)} %bitcast.place.refs_1_, s32[8,128]{1,0:T(8,128)S(1)} %get-tuple-element.35.refs_2_, f32[96,128]{1,0:T(8,128)S(1)} %collective-permute-done.12.refs_3_, f32[96,128]{1,0:T(8,128)S(1)} %collective-permute-done.13.refs_4_, ...), custom_call_target="tpu_custom_call" | custom-call | bytes 5242888 | tf_op jit(solution)/shard_map/pallas_call | solution.py:703
  (19 shorter events, 0.0 us)
Async XLA Ops:
  1.3 12.4 %copy-start.1 = (bf16[384,128]{1,0:T(8,128)(2,1)S(1)}, bf16[384,128]{1,0:T(8,128)(2,1)}, u32[]{:S(2)}) copy-start(bf16[384,128]{1,0:T(8,128)(2,1)} %constant.66.clone.refs_2_.refs_5_.refs_14_.refs_8_) | copy-start | bytes 294916
  1.3 12.4 %copy-start.2 = (f32[384,128]{1,0:T(8,128)S(1)}, f32[384,128]{1,0:T(8,128)}, u32[]{:S(2)}) copy-start(f32[384,128]{1,0:T(8,128)} %constant.67.clone.refs_6_.refs_9_.refs_19_) | copy-start | bytes 589828
  1.3 12.3 %copy-start.4 = (bf16[64,192]{1,0:T(8,128)(2,1)S(1)}, bf16[64,192]{1,0:T(8,128)(2,1)}, u32[]{:S(2)}) copy-start(bf16[64,192]{1,0:T(8,128)(2,1)} %constant.65.clone.refs_1_.refs_4_.refs_13_.refs_7_) | copy-start | bytes 73732
  1.3 12.3 %copy-start.6 = (bf16[128,256]{1,0:T(8,128)(2,1)S(1)}, bf16[128,256]{1,0:T(8,128)(2,1)}, u32[]{:S(2)}) copy-start(bf16[128,256]{1,0:T(8,128)(2,1)} %constant.68.clone.refs_7_.refs_10_) | copy-start | bytes 196612
  1.4 12.3 %copy-start.7 = (bf16[256,128]{1,0:T(8,128)(2,1)S(1)}, bf16[256,128]{1,0:T(8,128)(2,1)}, u32[]{:S(2)}) copy-start(bf16[256,128]{1,0:T(8,128)(2,1)} %constant.69.clone.refs_8_.refs_11_) | copy-start | bytes 196612
  1.4 12.3 %copy-start.10 = (bf16[16,256]{1,0:T(8,128)(2,1)S(1)}, bf16[16,256]{1,0:T(8,128)(2,1)}, u32[]{:S(2)}) copy-start(bf16[16,256]{1,0:T(8,128)(2,1)} %constant.60.clone.refs_0_.refs_3_.refs_6_) | copy-start | bytes 24580
  5.2 6.8 %collective-permute-start = (f32[96,128]{1,0:T(8,128)S(1)}, f32[96,128]{1,0:T(8,128)S(1)}, u32[]{:S(2)}, u32[]{:S(2)}) collective-permute-start(f32[96,128]{1,0:T(8,128)S(1)} %get-tuple-element.36), channel_id=1, source_target_pairs={{0,8},{1,4},{2,5},{3,6},{4,1},{5,2},{6,3},{7,15},{8,0},{9,12},{10,... | collective-permute-start | bytes 147464 | tf_op jit(solution)/shard_map/ppermute | solution.py:738
  8.2 6.7 %collective-permute-start.1 = (f32[96,128]{1,0:T(8,128)S(1)}, f32[96,128]{1,0:T(8,128)S(1)}, u32[]{:S(2)}, u32[]{:S(2)}) collective-permute-start(f32[96,128]{1,0:T(8,128)S(1)} %get-tuple-element.37), channel_id=1, source_target_pairs={{0,4},{1,5},{2,6},{3,7},{4,0},{5,1},{6,2},{7,3},{8,12},{9,13},{10,... | collective-permute-start | bytes 147464 | tf_op jit(solution)/shard_map/ppermute | solution.py:738
  8.4 6.5 %collective-permute-start.2 = (f32[96,128]{1,0:T(8,128)S(1)}, f32[96,128]{1,0:T(8,128)S(1)}, u32[]{:S(2)}, u32[]{:S(2)}) collective-permute-start(f32[96,128]{1,0:T(8,128)S(1)} %get-tuple-element.38), channel_id=1, source_target_pairs={{0,5},{1,6},{2,7},{3,11},{4,12},{5,0},{6,1},{7,2},{8,13},{9,14},{1... | collective-permute-start | bytes 147464 | tf_op jit(solution)/shard_map/ppermute | solution.py:738
  9.6 5.4 %collective-permute-start.3 = (f32[96,128]{1,0:T(8,128)S(1)}, f32[96,128]{1,0:T(8,128)S(1)}, u32[]{:S(2)}, u32[]{:S(2)}) collective-permute-start(f32[96,128]{1,0:T(8,128)S(1)} %get-tuple-element.39), channel_id=1, source_target_pairs={{0,29},{1,30},{2,31},{3,11},{4,12},{5,8},{6,9},{7,10},{8,5},{9,6},... | collective-permute-start | bytes 147464 | tf_op jit(solution)/shard_map/ppermute | solution.py:738
  12.0 4.4 %collective-permute-start.4 = (f32[96,128]{1,0:T(8,128)S(1)}, f32[96,128]{1,0:T(8,128)S(1)}, u32[]{:S(2)}, u32[]{:S(2)}) collective-permute-start(f32[96,128]{1,0:T(8,128)S(1)} %get-tuple-element.40), channel_id=1, source_target_pairs={{0,28},{1,29},{2,30},{3,31},{4,8},{5,9},{6,10},{7,11},{8,4},{9,5},... | collective-permute-start | bytes 147464 | tf_op jit(solution)/shard_map/ppermute | solution.py:738
  12.0 4.4 %collective-permute-start.5 = (f32[96,128]{1,0:T(8,128)S(1)}, f32[96,128]{1,0:T(8,128)S(1)}, u32[]{:S(2)}, u32[]{:S(2)}) collective-permute-start(f32[96,128]{1,0:T(8,128)S(1)} %get-tuple-element.41), channel_id=1, source_target_pairs={{0,1},{1,0},{2,29},{3,30},{4,9},{5,10},{6,11},{7,15},{8,16},{9,4},... | collective-permute-start | bytes 147464 | tf_op jit(solution)/shard_map/ppermute | solution.py:738
  13.7 2.7 %copy-start.3 = (f32[384,128]{1,0:T(8,128)S(1)}, f32[384,128]{1,0:T(8,128)}, u32[]{:S(2)}) copy-start(f32[384,128]{1,0:T(8,128)} %constant.62.clone.refs_10_) | copy-start | bytes 589828
  13.7 2.7 %copy-start.5 = (bf16[384,128]{1,0:T(8,128)(2,1)S(1)}, bf16[384,128]{1,0:T(8,128)(2,1)}, u32[]{:S(2)}) copy-start(bf16[384,128]{1,0:T(8,128)(2,1)} %constant.64.clone.refs_12_) | copy-start | bytes 294916
  13.7 2.7 %copy-start.9 = (bf16[64,192]{1,0:T(8,128)(2,1)S(1)}, bf16[64,192]{1,0:T(8,128)(2,1)}, u32[]{:S(2)}) copy-start(bf16[64,192]{1,0:T(8,128)(2,1)} %constant.63.clone.refs_11_) | copy-start | bytes 73732
  13.7 2.7 %copy-start.11 = (f32[8,128]{1,0:T(8,128)S(1)}, f32[8,128]{1,0:T(8,128)}, u32[]{:S(2)}) copy-start(f32[8,128]{1,0:T(8,128)} %constant.70.clone.refs_15_) | copy-start | bytes 12292
  13.8 12.4 %copy-start = (f32[128,4096]{1,0:T(8,128)S(1)}, f32[128,4096]{1,0:T(8,128)}, u32[]{:S(2)}) copy-start(f32[128,4096]{1,0:T(8,128)} %constant.59.clone.refs_4_.refs_17_) | copy-start | bytes 6291460
  13.8 12.4 %copy-start.8 = (bf16[128,32]{1,0:T(8,128)(2,1)S(1)}, bf16[128,32]{1,0:T(8,128)(2,1)}, u32[]{:S(2)}) copy-start(bf16[128,32]{1,0:T(8,128)(2,1)} %constant.61.clone.refs_5_.refs_18_) | copy-start | bytes 24580
  17.8 5.1 %collective-permute-start.6 = (f32[96,128]{1,0:T(8,128)S(1)}, f32[96,128]{1,0:T(8,128)S(1)}, u32[]{:S(2)}, u32[]{:S(2)}) collective-permute-start(f32[96,128]{1,0:T(8,128)S(1)} %get-tuple-element.46), channel_id=1, source_target_pairs={{0,8},{1,4},{2,5},{3,6},{4,1},{5,2},{6,3},{7,15},{8,0},{9,12},{10,... | collective-permute-start | bytes 147464 | tf_op jit(solution)/shard_map/ppermute | solution.py:738
  19.0 9.5 %collective-permute-start.7 = (f32[96,128]{1,0:T(8,128)S(1)}, f32[96,128]{1,0:T(8,128)S(1)}, u32[]{:S(2)}, u32[]{:S(2)}) collective-permute-start(f32[96,128]{1,0:T(8,128)S(1)} %get-tuple-element.47), channel_id=1, source_target_pairs={{0,4},{1,5},{2,6},{3,7},{4,0},{5,1},{6,2},{7,3},{8,12},{9,13},{10,... | collective-permute-start | bytes 147464 | tf_op jit(solution)/shard_map/ppermute | solution.py:738
  19.5 9.0 %collective-permute-start.8 = (f32[96,128]{1,0:T(8,128)S(1)}, f32[96,128]{1,0:T(8,128)S(1)}, u32[]{:S(2)}, u32[]{:S(2)}) collective-permute-start(f32[96,128]{1,0:T(8,128)S(1)} %get-tuple-element.48), channel_id=1, source_target_pairs={{0,5},{1,6},{2,7},{3,11},{4,12},{5,0},{6,1},{7,2},{8,13},{9,14},{1... | collective-permute-start | bytes 147464 | tf_op jit(solution)/shard_map/ppermute | solution.py:738
  22.1 6.5 %collective-permute-start.9 = (f32[96,128]{1,0:T(8,128)S(1)}, f32[96,128]{1,0:T(8,128)S(1)}, u32[]{:S(2)}, u32[]{:S(2)}) collective-permute-start(f32[96,128]{1,0:T(8,128)S(1)} %get-tuple-element.49), channel_id=1, source_target_pairs={{0,29},{1,30},{2,31},{3,11},{4,12},{5,8},{6,9},{7,10},{8,5},{9,6},... | collective-permute-start | bytes 147464 | tf_op jit(solution)/shard_map/ppermute | solution.py:738
  22.3 6.2 %collective-permute-start.10 = (f32[96,128]{1,0:T(8,128)S(1)}, f32[96,128]{1,0:T(8,128)S(1)}, u32[]{:S(2)}, u32[]{:S(2)}) collective-permute-start(f32[96,128]{1,0:T(8,128)S(1)} %get-tuple-element.50), channel_id=1, source_target_pairs={{0,28},{1,29},{2,30},{3,31},{4,8},{5,9},{6,10},{7,11},{8,4},{9,5},... | collective-permute-start | bytes 147464 | tf_op jit(solution)/shard_map/ppermute | solution.py:738
  22.9 5.7 %collective-permute-start.11 = (f32[96,128]{1,0:T(8,128)S(1)}, f32[96,128]{1,0:T(8,128)S(1)}, u32[]{:S(2)}, u32[]{:S(2)}) collective-permute-start(f32[96,128]{1,0:T(8,128)S(1)} %get-tuple-element.51), channel_id=1, source_target_pairs={{0,1},{1,0},{2,29},{3,30},{4,9},{5,10},{6,11},{7,15},{8,16},{9,4},... | collective-permute-start | bytes 147464 | tf_op jit(solution)/shard_map/ppermute | solution.py:738
  29.9 5.1 %collective-permute-start.12 = (f32[96,128]{1,0:T(8,128)S(1)}, f32[96,128]{1,0:T(8,128)S(1)}, u32[]{:S(2)}, u32[]{:S(2)}) collective-permute-start(f32[96,128]{1,0:T(8,128)S(1)} %get-tuple-element.55), channel_id=1, source_target_pairs={{0,8},{1,4},{2,5},{3,6},{4,1},{5,2},{6,3},{7,15},{8,0},{9,12},{10,... | collective-permute-start | bytes 147464 | tf_op jit(solution)/shard_map/ppermute | solution.py:738
  30.1 9.9 %collective-permute-start.13 = (f32[96,128]{1,0:T(8,128)S(1)}, f32[96,128]{1,0:T(8,128)S(1)}, u32[]{:S(2)}, u32[]{:S(2)}) collective-permute-start(f32[96,128]{1,0:T(8,128)S(1)} %get-tuple-element.56), channel_id=1, source_target_pairs={{0,4},{1,5},{2,6},{3,7},{4,0},{5,1},{6,2},{7,3},{8,12},{9,13},{10,... | collective-permute-start | bytes 147464 | tf_op jit(solution)/shard_map/ppermute | solution.py:738
  31.7 8.2 %collective-permute-start.14 = (f32[96,128]{1,0:T(8,128)S(1)}, f32[96,128]{1,0:T(8,128)S(1)}, u32[]{:S(2)}, u32[]{:S(2)}) collective-permute-start(f32[96,128]{1,0:T(8,128)S(1)} %get-tuple-element.57), channel_id=1, source_target_pairs={{0,5},{1,6},{2,7},{3,11},{4,12},{5,0},{6,1},{7,2},{8,13},{9,14},{1... | collective-permute-start | bytes 147464 | tf_op jit(solution)/shard_map/ppermute | solution.py:738
  33.5 6.5 %collective-permute-start.15 = (f32[96,128]{1,0:T(8,128)S(1)}, f32[96,128]{1,0:T(8,128)S(1)}, u32[]{:S(2)}, u32[]{:S(2)}) collective-permute-start(f32[96,128]{1,0:T(8,128)S(1)} %get-tuple-element.58), channel_id=1, source_target_pairs={{0,29},{1,30},{2,31},{3,11},{4,12},{5,8},{6,9},{7,10},{8,5},{9,6},... | collective-permute-start | bytes 147464 | tf_op jit(solution)/shard_map/ppermute | solution.py:738
  33.5 6.5 %collective-permute-start.16 = (f32[96,128]{1,0:T(8,128)S(1)}, f32[96,128]{1,0:T(8,128)S(1)}, u32[]{:S(2)}, u32[]{:S(2)}) collective-permute-start(f32[96,128]{1,0:T(8,128)S(1)} %get-tuple-element.59), channel_id=1, source_target_pairs={{0,28},{1,29},{2,30},{3,31},{4,8},{5,9},{6,10},{7,11},{8,4},{9,5},... | collective-permute-start | bytes 147464 | tf_op jit(solution)/shard_map/ppermute | solution.py:738
  34.9 5.1 %collective-permute-start.17 = (f32[96,128]{1,0:T(8,128)S(1)}, f32[96,128]{1,0:T(8,128)S(1)}, u32[]{:S(2)}, u32[]{:S(2)}) collective-permute-start(f32[96,128]{1,0:T(8,128)S(1)} %get-tuple-element.60), channel_id=1, source_target_pairs={{0,1},{1,0},{2,29},{3,30},{4,9},{5,10},{6,11},{7,15},{8,16},{9,4},... | collective-permute-start | bytes 147464 | tf_op jit(solution)/shard_map/ppermute | solution.py:738
